TPU v7x, 32 devices: a whole 2x2x4 slice. The times are simulated.
32 devices in a mesh: shard: 4 (over z), ctx: 4 (over x, core), tp: 2 (over y).
Axes of the slice: x: 2, y: 2, z: 4, core: 2. Of those that a mesh axis runs over, the one named last changes fastest.
Arguments:
- inputs: bfloat16 [4, 2048, 2048], P('shard', 'ctx'), may hold values from -6 to 6
- output_grad: bfloat16 [4, 2048, 2048], P('shard', 'ctx'), may hold values from -6 to 6
- seq_lengths: int32 [4], P('shard'), may hold values from 1537 to 2048, as said below
- attn_gain: bfloat16 [2048], P('shard'), may hold values from 0.5 to 1.5
- query_weight: bfloat16 [2048, 2048], P('shard', 'tp'), may hold values from -0.125 to 0.125
- key_matrix: bfloat16 [2048, 512], P('shard', 'tp'), may hold values from -0.125 to 0.125
- value_matrix: bfloat16 [2048, 512], P('shard', 'tp'), may hold values from -0.125 to 0.125
- out_weight: bfloat16 [2048, 2048], P('tp', 'shard'), may hold values from -0.5 to 0.5
- query_adapter_input: bfloat16 [2048, 8], P('shard'), may hold values from -0.125 to 0.125
- query_up: bfloat16 [8, 32, 64], P(None, 'tp', 'shard'), may hold values from -1 to 1
- key_adapter_input: bfloat16 [2048, 8], P('shard'), may hold values from -0.125 to 0.125
- key_adapter_output: bfloat16 [8, 8, 64], P(None, 'tp', 'shard'), may hold values from -1 to 1
- value_adapter_input: bfloat16 [2048, 8], P('shard'), may hold values from -0.125 to 0.125
- value_adapter_output: bfloat16 [8, 8, 64], P(None, 'tp', 'shard'), may hold values from -1 to 1
- out_down: bfloat16 [32, 64, 8], P('tp', 'shard'), may hold values from -0.125 to 0.125
- out_up: bfloat16 [8, 2048], P(None, 'shard'), may hold values from -3 to 3
- query_map: bfloat16 [32, 64, 64], P('tp', 'shard'), may hold values from -0.75 to 0.75
- key_feature_map: bfloat16 [8, 64, 64], P('tp', 'shard'), may hold values from -0.75 to 0.75
- ffn_gain: bfloat16 [2048], P('shard'), may hold values from 0.5 to 1.5
- gate_weight: bfloat16 [2048, 8192], P('shard', 'tp'), may hold values from -0.125 to 0.125
- up_weight: bfloat16 [2048, 8192], P('shard', 'tp'), may hold values from -0.125 to 0.125
- down_weight: bfloat16 [8192, 2048], P('tp', 'shard'), may hold values from -0.0625 to 0.0625
Outputs:
- outputs: bfloat16 [4, 2048, 2048], P('shard', 'ctx')
- input_grad: float32 [4, 2048, 2048], P('shard', 'ctx')
- attn_gain_grad: float32 [2048], P('shard')
- query_weight_grad: float32 [2048, 2048], P('shard', 'tp')
- key_weight_grad: float32 [2048, 512], P('shard', 'tp')
- value_weight_grad: float32 [2048, 512], P('shard', 'tp')
- out_weight_grad: float32 [2048, 2048], P('tp', 'shard')
- query_down_grad: float32 [2048, 8], P('shard')
- query_up_grad: float32 [8, 32, 64], P(None, 'tp', 'shard')
- key_down_grad: float32 [2048, 8], P('shard')
- key_up_grad: float32 [8, 8, 64], P(None, 'tp', 'shard')
- value_down_grad: float32 [2048, 8], P('shard')
- value_up_grad: float32 [8, 8, 64], P(None, 'tp', 'shard')
- out_down_grad: float32 [32, 64, 8], P('tp', 'shard')
- out_up_grad: float32 [8, 2048], P(None, 'shard')
- query_map_grad: float32 [32, 64, 64], P('tp', 'shard')
- key_map_grad: float32 [8, 64, 64], P('tp', 'shard')
- ffn_gain_grad: float32 [2048], P('shard')
- gate_weight_grad: float32 [2048, 8192], P('shard', 'tp')
- up_weight_grad: float32 [2048, 8192], P('shard', 'tp')
- down_weight_grad: float32 [8192, 2048], P('tp', 'shard')
Inputs may be any that keep to these rules, and one draw needn't show every extreme that they name: `seq_lengths`: one sequence in every draw fills all 2048 slots.
All inputs are finite; a program needn't handle non-finite values.
Results may differ from a plain program's by a relative error of at most 0.023.
Values may be sent and summed in bfloat16 or wider, within the bound.
No kernel may reach another device: no remote copies, remote signals or barrier semaphores. Data moves between devices by JAX's collectives and lax.ppermute only.
A program may use at most 320 MiB of HBM per device.

v0:
```python
import functools

import jax
import jax.numpy as jnp
import numpy as np
from jax import lax
from jax.experimental import pallas as pl
from jax.experimental.pallas import tpu as pltpu
from jax.sharding import PartitionSpec as P

BLOCK = 64
EPSILON = 1e-05
ROPE_BASE = 500000.0
SCALE = 0.125
BF = jnp.bfloat16
F32 = jnp.float32

CORE = [(c, c ^ 1) for c in range(4)]
ALONG_X = [(c, c ^ 2) for c in range(4)]
ALONG_Y = [(0, 1), (1, 0)]


def dot(a, b):
    return jnp.dot(a, b, preferred_element_type=F32)


def dot_nt(a, b):
    return lax.dot_general(a, b, (((1,), (1,)), ((), ())), preferred_element_type=F32)


def dot_tn(a, b):
    return lax.dot_general(a, b, (((0,), (0,)), ((), ())), preferred_element_type=F32)


def to_core(a):
    return lax.ppermute(a, "ctx", CORE)


def to_x(a):
    return lax.ppermute(a, "ctx", ALONG_X)


def to_y(a):
    return lax.ppermute(a, "tp", ALONG_Y)


def gather_plane(own, y_piece=None):
    half = own.shape[0] // 2
    px = to_x(own)
    py = to_y(own) if y_piece is None else y_piece
    c0 = to_core(own)
    bxy = to_x(py[half:])
    axy = to_y(px[:half])
    cx, cy = to_core(px), to_core(py)
    caxy, cbxy = to_core(axy), to_core(bxy)
    return jnp.concatenate([own, px, py, axy, bxy, c0, cx, cy, caxy, cbxy], axis=0)


def scatter_plane(away, here):
    rows, n = here.shape[0] // 4, here.shape[1]
    got = to_core(away)
    s = (here.astype(F32) + got.astype(F32)).reshape(4, 2, rows // 2, n)
    low = s.astype(BF)
    r3a, r3b = to_x(low[3, 0]), to_y(low[3, 1])
    r1a, r2b = to_x(low[1, 0]), to_y(low[2, 1])
    r1b = to_x((s[1, 1] + r3b.astype(F32)).astype(BF))
    r2a = to_y((s[2, 0] + r3a.astype(F32)).astype(BF))
    return jnp.concatenate(
        [
            s[0, 0] + r1a.astype(F32) + r2a.astype(F32),
            s[0, 1] + r1b.astype(F32) + r2b.astype(F32),
        ],
        axis=0,
    )


def stack(m, heads):
    return jnp.concatenate([m[:, h * 64 : (h + 1) * 64] for h in range(heads)], axis=0)


def unstack(m, heads):
    rows = m.shape[0] // heads
    return jnp.concatenate([m[h * rows : (h + 1) * rows] for h in range(heads)], axis=1)


def turned(v, cos, sin):
    first = lax.broadcasted_iota(jnp.int32, v.shape, 1) % 64 < 32
    return v * cos + jnp.where(first, pltpu.roll(v, 96, 1), pltpu.roll(v, 32, 1)) * sin


def key_tables(cos, sin):
    low = lax.broadcasted_iota(jnp.int32, cos.shape, 1) < 64
    return jnp.where(low, cos, 1.0), jnp.where(low, sin, 0.0)


def two_softmaxes(logit):
    both = jnp.concatenate([logit, -logit], axis=1)
    low = lax.broadcasted_iota(jnp.int32, both.shape, 1) < 64
    top = jnp.where(
        low,
        jnp.max(logit, axis=1, keepdims=True),
        jnp.max(-logit, axis=1, keepdims=True),
    )
    e = jnp.exp(both - top)
    first = jnp.sum(jnp.where(low, e, 0.0), axis=1, keepdims=True)
    second = jnp.sum(jnp.where(low, 0.0, e), axis=1, keepdims=True)
    return e * jnp.where(low, 1.0 / first, 1.0 / second)


def two_softmaxes_back(feat, grad):
    w = feat * grad
    low = lax.broadcasted_iota(jnp.int32, w.shape, 1) < 64
    first = jnp.sum(jnp.where(low, w, 0.0), axis=1, keepdims=True)
    second = jnp.sum(jnp.where(low, 0.0, w), axis=1, keepdims=True)
    y = w - feat * jnp.where(low, first, second)
    return (y - pltpu.roll(y, 64, 1))[:, :64]


def forward_kernel(
    heads,
    perm,
    length,
    lin_ref,
    cos_ref,
    sin_ref,
    mq_ref,
    mk_ref,
    mixlow_ref,
    mix_ref,
    rden_ref,
    q_ref,
    kv_ref,
    qf_ref,
    kf_ref,
    a_ref,
    st_ref,
    n_ref,
    kvp,
    fp,
    st,
    nr,
):
    i = pl.program_id(0)
    rows = lin_ref.shape[0]
    blocks = rows // BLOCK
    wide = heads * 64

    @pl.when(i == 0)
    def _():
        kvp[...] = jnp.zeros_like(kvp)
        fp[...] = jnp.zeros_like(fp)
        st[...] = jnp.zeros_like(st)
        nr[...] = jnp.zeros_like(nr)

    seq = length[0]
    cos, sin = cos_ref[...], sin_ref[...]
    q_low = jnp.concatenate(
        [
            turned(lin_ref[:, p * 128 : (p + 1) * 128], cos, sin).astype(BF)
            for p in range(wide // 128)
        ],
        axis=1,
    )
    kv_low = turned(lin_ref[:, wide:], *key_tables(cos, sin)).astype(BF)
    q_ref[...] = q_low
    kv_ref[...] = kv_low
    q_logit = dot(q_low, mq_ref[...])
    k_logit = dot(kv_low[:, :64], mk_ref[...])
    for h in range(heads):
        feat = two_softmaxes(q_logit[:, h * 64 : (h + 1) * 64])
        for j in range(blocks):
            at = (j * heads + h) * BLOCK
            qf_ref[at : at + BLOCK, :] = feat[j * BLOCK : (j + 1) * BLOCK]
    kf = two_softmaxes(k_logit)
    kf_ref[...] = kf
    pos = i * rows + lax.broadcasted_iota(jnp.int32, kf.shape, 0)
    kf_low = jnp.where(pos < seq, kf, 0.0).astype(BF)

    span = heads * BLOCK
    off = lax.broadcasted_iota(jnp.int32, (span, 128), 0) % BLOCK
    lane = lax.broadcasted_iota(jnp.int32, (span, 128), 1)
    near_at = lane <= off
    near_at = near_at & (lane < 64)
    prob_at = (lane > off) & (lane - 64 <= off)
    zero = jnp.zeros((BLOCK, 128), BF)
    for j in range(blocks):
        r = slice(j * BLOCK, (j + 1) * BLOCK)
        before = slice((j - 1) * BLOCK, j * BLOCK)
        kv_prev = kvp[...] if j == 0 else kv_low[before]
        f_prev = fp[...] if j == 0 else kf_low[before]
        kv2 = jnp.concatenate([kv_prev, kv_low[r]], axis=0)
        k2, v2 = kv2[:, :64], kv2[:, 64:]
        q = stack(q_low[r], heads)
        qf = qf_ref[j * span : (j + 1) * span, :].astype(BF)
        st_low = st[...].astype(BF)
        norm = nr[...]
        score = dot_nt(q, k2)
        near = dot_nt(qf, jnp.concatenate([f_prev, zero], axis=0))
        key_pos = (i * blocks + j - 1) * BLOCK + lane
        live = prob_at & (key_pos >= 0) & (key_pos < seq)
        a = jnp.where(near_at, near, jnp.where(live, jnp.exp(SCALE * score), 0.0))
        numer = dot(a.astype(BF), v2) + dot_nt(qf, st_low)
        denom = jnp.sum(a + qf.astype(F32) * norm, axis=1, keepdims=True)
        rden = 1.0 / denom
        mixed = unstack(numer * rden, heads)
        a_ref[j * span : (j + 1) * span, :] = a
        mix_ref[r, :] = mixed
        mixlow_ref[r, :] = mixed.astype(BF)
        rden_ref[r, :] = unstack(jnp.broadcast_to(rden, (span, 64)), heads)
        st_ref[r, :] = st_low
        n_ref[0, j : j + 1, :] = norm
        st[...] += dot_tn(kv_prev[:, 64:], f_prev)
        nr[...] += jnp.sum(f_prev.astype(F32), axis=0, keepdims=True)
    last = slice((blocks - 1) * BLOCK, blocks * BLOCK)
    kvp[...] = kv_low[last]
    fp[...] = kf_low[last]


def backward_kernel(
    heads,
    perm,
    length,
    dmix_ref,
    mix_ref,
    rden_ref,
    q_ref,
    kv_ref,
    kvb_ref,
    qf_ref,
    kf_ref,
    kfb_ref,
    a_ref,
    st_ref,
    n_ref,
    cos_ref,
    sin_ref,
    mq_ref,
    mk_ref,
    dlin_ref,
    dmq_ref,
    dmk_ref,
    carry,
    carry_f,
    rt,
    rn,
    dq_s,
    dql_s,
    dkv_s,
    df_s,
):
    g = pl.program_id(0)
    i = pl.num_programs(0) - 1 - g
    rows = dmix_ref.shape[0]
    blocks = rows // BLOCK
    wide = heads * 64

    @pl.when(g == 0)
    def _():
        carry[...] = jnp.zeros_like(carry)
        carry_f[...] = jnp.zeros_like(carry_f)
        rt[...] = jnp.zeros_like(rt)
        rn[...] = jnp.zeros_like(rn)
        dmq_ref[...] = jnp.zeros_like(dmq_ref)
        dmk_ref[...] = jnp.zeros_like(dmk_ref)

    seq = length[0]
    kf = kf_ref[...]
    row = lax.broadcasted_iota(jnp.int32, kf.shape, 0)
    valid = i * rows + row < seq
    kf_low = jnp.where(valid, kf, 0.0).astype(BF)
    row_b = lax.broadcasted_iota(jnp.int32, (BLOCK, 128), 0)
    valid_b = (i > 0) & (i * rows - BLOCK + row_b < seq)
    f_first = jnp.where(valid_b, kfb_ref[...], 0.0).astype(BF)
    kv_first = jnp.where(i > 0, kvb_ref[...].astype(F32), 0.0).astype(BF)

    span = heads * BLOCK
    off = lax.broadcasted_iota(jnp.int32, (span, 128), 0) % BLOCK
    lane = lax.broadcasted_iota(jnp.int32, (span, 128), 1)
    near_at = (lane <= off) & (lane < 64)
    no_q = jnp.zeros((span, 64), BF)
    for j in reversed(range(blocks)):
        r = slice(j * BLOCK, (j + 1) * BLOCK)
        before = slice((j - 1) * BLOCK, j * BLOCK)
        kv_prev = kv_first if j == 0 else kv_ref[before, :]
        f_prev = f_first if j == 0 else kf_low[before]
        kv2 = jnp.concatenate([kv_prev, kv_ref[r, :]], axis=0)
        k2, v2 = kv2[:, :64], kv2[:, 64:]
        q = stack(q_ref[r, :], heads)
        feat = qf_ref[j * span : (j + 1) * span, :]
        qf = feat.astype(BF)
        a = a_ref[j * span : (j + 1) * span, :]
        st_low = st_ref[r, :]
        norm = n_ref[0, j : j + 1, :]
        ng_rows = dmix_ref[r, :] * rden_ref[r, :]
        ng32 = stack(ng_rows, heads)
        dg = -jnp.sum(stack(ng_rows * mix_ref[r, :], heads), axis=1, keepdims=True)
        ng = ng32.astype(BF)
        pull = dot_nt(ng, v2) + dg
        sg = jnp.where(near_at, 0.0, pull * a).astype(BF)
        near_g = jnp.where(near_at, pull, 0.0).astype(BF)[:, :64]
        x = jnp.concatenate([near_g, ng], axis=1)
        dq_s[r, :] = unstack(SCALE * dot(sg, k2), heads)
        dkv2 = SCALE * dot_tn(sg, jnp.concatenate([q, no_q], axis=1)) + dot_tn(
            a.astype(BF), jnp.concatenate([no_q, ng], axis=1)
        )
        dqf = dot(x, jnp.concatenate([f_prev, st_low], axis=0)) + dg * norm
        xf = dot_tn(x, qf)
        rt_low = rt[...].astype(BF)
        dkv_s[r, :] = dkv2[BLOCK:] + carry[...]
        df_s[r, :] = carry_f[...]
        dv_state = dot_nt(f_prev, rt_low)
        carry[...] = dkv2[:BLOCK] + jnp.concatenate([jnp.zeros((BLOCK, 64), F32), dv_state], axis=1)
        carry_f[...] = xf[:64] + dot(kv_prev[:, 64:], rt_low) + rn[...]
        rt[...] += xf[64:]
        rn[...] += jnp.sum(dg * qf.astype(F32), axis=0, keepdims=True)
        dql_s[r, :] = unstack(two_softmaxes_back(feat, dqf).astype(BF), heads)

    cos, sin = cos_ref[...], -sin_ref[...]
    dql = dql_s[...]
    dmq_ref[...] += dot_tn(q_ref[...], dql)
    dq = dq_s[...] + dot_nt(dql, mq_ref[...])
    for p in range(wide // 128):
        at = slice(p * 128, (p + 1) * 128)
        dlin_ref[:, at] = turned(dq[:, at], cos, sin).astype(BF)
    dkl = two_softmaxes_back(kf, jnp.where(valid, df_s[...], 0.0)).astype(BF)
    dmk_ref[...] += dot_tn(kv_ref[:, :64], dkl)
    dk_map = dot_nt(dkl, mk_ref[...])
    dkv = dkv_s[...] + jnp.concatenate([dk_map, jnp.zeros_like(dk_map)], axis=1)
    dlin_ref[:, wide:] = turned(dkv, *key_tables(cos, sin)).astype(BF)


def attention_forward(lin, cos, sin, mq, mk, perm, seq_lengths):
    slots, cols = lin.shape
    heads = (cols - 128) // 64
    pieces = perm.shape[0]
    rows = slots // pieces
    blocks = rows // BLOCK
    wide = heads * 64
    span = heads * rows
    moved = lambda i, perm, length: (perm[i], 0)
    plain = lambda i, perm, length: (i, 0)
    fixed = lambda i, perm, length: (0, 0)
    grid = pltpu.PrefetchScalarGridSpec(
        num_scalar_prefetch=2,
        grid=(pieces,),
        in_specs=[
            pl.BlockSpec((rows, cols), moved),
            pl.BlockSpec((rows, 128), plain),
            pl.BlockSpec((rows, 128), plain),
            pl.BlockSpec((wide, wide), fixed),
            pl.BlockSpec((64, 64), fixed),
        ],
        out_specs=[
            pl.BlockSpec((rows, wide), moved),
            pl.BlockSpec((rows, wide), plain),
            pl.BlockSpec((rows, wide), plain),
            pl.BlockSpec((rows, wide), plain),
            pl.BlockSpec((rows, 128), plain),
            pl.BlockSpec((span, 128), plain),
            pl.BlockSpec((rows, 128), plain),
            pl.BlockSpec((span, 128), plain),
            pl.BlockSpec((rows, 128), plain),
            pl.BlockSpec((1, 8, 128), lambda i, perm, length: (i, 0, 0)),
        ],
        scratch_shapes=[
            pltpu.VMEM((BLOCK, 128), BF),
            pltpu.VMEM((BLOCK, 128), BF),
            pltpu.VMEM((64, 128), F32),
            pltpu.VMEM((1, 128), F32),
        ],
    )
    made = lambda *s: jax.ShapeDtypeStruct(s[:-1], s[-1])
    return pl.pallas_call(
        functools.partial(forward_kernel, heads),
        grid_spec=grid,
        out_shape=[
            made(slots, wide, BF),
            made(slots, wide, F32),
            made(slots, wide, F32),
            made(slots, wide, BF),
            made(slots, 128, BF),
            made(slots * heads, 128, F32),
            made(slots, 128, F32),
            made(slots * heads, 128, F32),
            made(slots, 128, BF),
            made(pieces, 8, 128, F32),
        ],
        compiler_params=pltpu.CompilerParams(vmem_limit_bytes=48 << 20),
        cost_estimate=pl.CostEstimate(flops=10**10, bytes_accessed=20 << 20, transcendentals=1 << 22),
        name="attention_forward",
    )(perm, seq_lengths, lin, cos, sin, mq, mk)


def attention_backward(dmix, saved, cos, sin, mq, mk, perm, seq_lengths):
    mix, rden, q, kv, qf, kf, a, st, norm = saved
    slots, wide = dmix.shape
    heads = wide // 64
    pieces = perm.shape[0]
    rows = slots // pieces
    blocks = rows // BLOCK
    span = heads * rows
    last = pieces - 1
    moved = lambda g, perm, length: (perm[last - g], 0)
    plain = lambda g, perm, length: (last - g, 0)
    prior = lambda g, perm, length: (jnp.maximum((last - g) * blocks - 1, 0), 0)
    fixed = lambda g, perm, length: (0, 0)
    grid = pltpu.PrefetchScalarGridSpec(
        num_scalar_prefetch=2,
        grid=(pieces,),
        in_specs=[
            pl.BlockSpec((rows, wide), moved),
            pl.BlockSpec((rows, wide), plain),
            pl.BlockSpec((rows, wide), plain),
            pl.BlockSpec((rows, wide), plain),
            pl.BlockSpec((rows, 128), plain),
            pl.BlockSpec((BLOCK, 128), prior),
            pl.BlockSpec((span, 128), plain),
            pl.BlockSpec((rows, 128), plain),
            pl.BlockSpec((BLOCK, 128), prior),
            pl.BlockSpec((span, 128), plain),
            pl.BlockSpec((rows, 128), plain),
            pl.BlockSpec((1, 8, 128), lambda g, perm, length: (last - g, 0, 0)),
            pl.BlockSpec((rows, 128), plain),
            pl.BlockSpec((rows, 128), plain),
            pl.BlockSpec((wide, wide), fixed),
            pl.BlockSpec((64, 64), fixed),
        ],
        out_specs=[
            pl.BlockSpec((rows, wide + 128), moved),
            pl.BlockSpec((wide, wide), fixed),
            pl.BlockSpec((64, 64), fixed),
        ],
        scratch_shapes=[
            pltpu.VMEM((BLOCK, 128), F32),
            pltpu.VMEM((BLOCK, 128), F32),
            pltpu.VMEM((64, 128), F32),
            pltpu.VMEM((1, 128), F32),
            pltpu.VMEM((rows, wide), F32),
            pltpu.VMEM((rows, wide), BF),
            pltpu.VMEM((rows, 128), F32),
            pltpu.VMEM((rows, 128), F32),
        ],
    )
    return pl.pallas_call(
        functools.partial(backward_kernel, heads),
        grid_spec=grid,
        out_shape=[
            jax.ShapeDtypeStruct((slots, wide + 128), BF),
            jax.ShapeDtypeStruct((wide, wide), F32),
            jax.ShapeDtypeStruct((64, 64), F32),
        ],
        compiler_params=pltpu.CompilerParams(vmem_limit_bytes=48 << 20),
        cost_estimate=pl.CostEstimate(flops=2 * 10**10, bytes_accessed=20 << 20, transcendentals=0),
        name="attention_backward",
    )(perm, seq_lengths, dmix, mix, rden, q, kv, kv, qf, kf, kf, a, st, norm, cos, sin, mq, mk)


def place_kernel(turn, at, *refs):
    pieces, outs = refs[:4], refs[4:]
    p = pl.program_id(0)
    for k in range(4):

        @pl.when(p == k)
        def _(k=k):
            left = 0
            for out in outs:
                if turn:
                    out[...] = pieces[k][...].astype(F32).T
                else:
                    wide = out.shape[1]
                    out[...] = pieces[k][:, left : left + wide].astype(F32)
                    left += wide


def place(pieces, here, splits, turn=False):
    rows, cols = pieces[0].shape
    tile = min(rows, 128)
    steps = rows // tile

    def taken(k):
        return lambda p, i, at: (jnp.where(p == k, i, jnp.where(p > k, steps - 1, 0)), 0)

    if turn:
        out_specs = [pl.BlockSpec((cols, tile), lambda p, i, at: (p ^ at[0], i))]
        out_shape = [jax.ShapeDtypeStruct((4 * cols, rows), F32)]
    else:
        out_specs = [pl.BlockSpec((tile, s), lambda p, i, at: (i, p ^ at[0])) for s in splits]
        out_shape = [jax.ShapeDtypeStruct((rows, 4 * s), F32) for s in splits]
    return pl.pallas_call(
        functools.partial(place_kernel, turn),
        grid_spec=pltpu.PrefetchScalarGridSpec(
            num_scalar_prefetch=1,
            grid=(4, steps),
            in_specs=[pl.BlockSpec((tile, cols), taken(k)) for k in range(4)],
            out_specs=out_specs,
        ),
        out_shape=out_shape,
        compiler_params=pltpu.CompilerParams(vmem_limit_bytes=32 << 20),
        name="place",
    )(here, *pieces)


def on_ctx(own):
    ax = to_x(own)
    return [own, to_core(own), ax, to_core(ax)]


def absolute(pieces, x, k):
    swap = k == 1
    a0, a1 = jnp.where(swap, pieces[1], pieces[0]), jnp.where(swap, pieces[0], pieces[1])
    a2, a3 = jnp.where(swap, pieces[3], pieces[2]), jnp.where(swap, pieces[2], pieces[3])
    over = x == 1
    return [
        jnp.where(over, a2, a0),
        jnp.where(over, a3, a1),
        jnp.where(over, a0, a2),
        jnp.where(over, a1, a3),
    ]


def on_diagonal(blocks):
    n, a, b = blocks.shape
    eye = jnp.eye(n, dtype=blocks.dtype)
    return (eye[:, None, :, None] * blocks[:, :, None, :]).reshape(n * a, n * b)


def body(
    inputs,
    output_grad,
    seq_lengths,
    attn_gain,
    query_weight,
    key_matrix,
    value_matrix,
    out_weight,
    query_adapter_input,
    query_up,
    key_adapter_input,
    key_adapter_output,
    value_adapter_input,
    value_adapter_output,
    out_down,
    out_up,
    query_map,
    key_feature_map,
    ffn_gain,
    gate_weight,
    up_weight,
    down_weight,
):
    shards = lax.axis_size("shard")
    c, t, s = lax.axis_index("ctx"), lax.axis_index("tp"), lax.axis_index("shard")
    x, k = c // 2, c % 2
    tokens, width = inputs.shape[1:]
    piece = tokens // 2
    slots = tokens * 4
    ds = width // shards
    rank = query_adapter_input.shape[1]
    hs = query_map.shape[1]
    heads = query_map.shape[0] // 4
    wide = heads * 64
    units = gate_weight.shape[1] // 4

    def mine(a, dim):
        return lax.dynamic_slice_in_dim(a, c * (a.shape[dim] // 4), a.shape[dim] // 4, dim)

    def gathered(a):
        return lax.all_gather(a, "shard", axis=0, tiled=True)

    rows_in = lax.dynamic_slice_in_dim(inputs[0], t * piece, piece, 0)
    rows_in_y = lax.dynamic_slice_in_dim(inputs[0], (1 - t) * piece, piece, 0)
    pos = c * tokens + jnp.arange(tokens, dtype=jnp.int32)
    cot_all = jnp.where((pos < seq_lengths[0])[:, None], output_grad[0], 0).astype(BF)
    cot_own = lax.dynamic_slice_in_dim(cot_all, t * piece, piece, 0)
    cot_y = lax.dynamic_slice_in_dim(cot_all, (1 - t) * piece, piece, 0)

    flat = lambda a: a.reshape(-1, ds)
    ups_small = jnp.concatenate(
        [mine(key_adapter_output, 1).reshape(-1), mine(value_adapter_output, 1).reshape(-1)]
    )
    small = jnp.concatenate(
        [
            query_adapter_input.T,
            key_adapter_input.T,
            value_adapter_input.T,
            out_up,
            attn_gain[None],
            ffn_gain[None],
            flat(mine(query_up, 1)),
            jnp.concatenate([ups_small, jnp.zeros_like(ups_small)])[None],
            flat(mine(out_down, 0)),
            flat(mine(query_map, 0)),
            flat(mine(key_feature_map, 0)),
            jnp.zeros((1, ds), BF),
        ],
        axis=0,
    )
    small_all = lax.all_gather(small, "shard", axis=0)
    downs = small_all[:, : 3 * rank].transpose(1, 0, 2).reshape(3 * rank, width)
    out_up_all = small_all[:, 24:32].transpose(1, 0, 2).reshape(rank, width)
    gain_one = small_all[:, 32].reshape(width).astype(F32)
    gain_two = small_all[:, 33].reshape(width).astype(F32)
    query_up_all = small_all[:, 34].reshape(shards, rank, heads, hs).transpose(1, 2, 0, 3).reshape(rank, wide)
    both_up = small_all[:, 35, : ds // 2].reshape(shards, 2, rank, hs).transpose(1, 2, 0, 3).reshape(2, rank, 64)
    out_down_all = small_all[:, 36].reshape(shards, heads, hs, rank).transpose(1, 0, 2, 3).reshape(wide, rank)
    maps_q = small_all[:, 37:45].reshape(shards, heads, hs, 64).transpose(1, 0, 2, 3).reshape(heads, 64, 64)
    mk = small_all[:, 45:47].reshape(64, 64)
    mq = on_diagonal(maps_q)
    ups = jnp.zeros((3 * rank, wide + 128), BF)
    ups = ups.at[:rank, :wide].set(query_up_all)
    ups = ups.at[rank : 2 * rank, wide : wide + 64].set(both_up[0])
    ups = ups.at[2 * rank :, wide + 64 :].set(both_up[1])

    w_in_own = jnp.concatenate([mine(query_weight, 1), mine(key_matrix, 1), mine(value_matrix, 1)], axis=1)
    w_in = gathered(w_in_own)
    w_out = lax.all_gather(mine(out_weight, 0), "shard", axis=0)
    w_gu_own = jnp.concatenate([mine(gate_weight, 1), mine(up_weight, 1)], axis=1)
    w_gu = gathered(w_gu_own)
    w_dt = gathered(mine(down_weight, 0).T)

    w_in_eff = (w_in.astype(F32) + dot_tn(downs, ups)).astype(BF)
    w_out_eff = (
        w_out.transpose(1, 0, 2).reshape(wide, width).astype(F32) + dot(out_down_all, out_up_all)
    ).astype(BF)

    h_in = gather_plane(rows_in, rows_in_y)
    cot = gather_plane(cot_own, cot_y)

    inv_freq = ROPE_BASE ** (-(np.arange(32, dtype=np.float64) * 2.0) / 64)
    angle = np.arange(slots, dtype=np.float64)[:, None] * inv_freq[None, :]
    cos = jnp.asarray(np.tile(np.cos(angle), (1, 4)), F32)
    sin = jnp.asarray(np.tile(np.concatenate([-np.sin(angle), np.sin(angle)], 1), (1, 2)), F32)
    order = np.arange(8)
    perm = (((order >> 1) & 1) ^ k) * 4 + ((order & 1) ^ t) * 2 + ((order >> 2) ^ x)
    perm = perm.astype(jnp.int32)

    def scale_of(rows):
        return lax.rsqrt(jnp.mean(rows * rows, axis=-1, keepdims=True) + EPSILON)

    h_wide = h_in.astype(F32)
    normed = (h_wide * scale_of(h_wide) * gain_one).astype(BF)
    lin = dot(normed, w_in_eff)
    mixed, *saved = attention_forward(lin, cos, sin, mq, mk, perm, seq_lengths)

    half = slots // 2
    out_away = dot(mixed[half:], w_out_eff).astype(BF)
    out_here = dot(mixed[:half], w_out_eff).astype(BF)
    middle = rows_in.astype(F32) + scatter_plane(out_away, out_here)
    scale_two = scale_of(middle)
    normed_two_own = (middle * scale_two * gain_two).astype(BF)
    normed_two = gather_plane(normed_two_own)

    gu = dot(normed_two, w_gu)
    gate, up = gu[:, :units], gu[:, units:]
    sig = jax.nn.sigmoid(gate)
    silu = gate * sig
    active = (silu * up).astype(BF)
    active_grad = dot(cot, w_dt)
    gu_grad = jnp.concatenate(
        [
            (active_grad * up * (sig * (1.0 + gate * (1.0 - sig)))).astype(BF),
            (active_grad * silu).astype(BF),
        ],
        axis=1,
    )
    n2g_away = dot_nt(gu_grad[half:], w_gu).astype(BF)
    n2g_here = dot_nt(gu_grad[:half], w_gu).astype(BF)
    normed_two_grad = scatter_plane(n2g_away, n2g_here)

    ffn_away = dot_nt(active[half:], w_dt).astype(BF)
    ffn_here = dot_nt(active[:half], w_dt).astype(BF)
    out_own = (middle + scatter_plane(ffn_away, ffn_here)).astype(BF)

    def both_tp(own):
        other = to_y(own)
        first = t == 0
        return jnp.concatenate([jnp.where(first, own, other), jnp.where(first, other, own)], axis=0)

    outputs = both_tp(out_own)[None]

    dw_dt = dot_tn(cot, active).astype(BF)
    dw_gu = dot_tn(normed_two, gu_grad).astype(BF)

    def scattered(a):
        return lax.psum_scatter(a, "shard", scatter_dimension=0, tiled=True)

    dw_dt_own = scattered(dw_dt)
    dw_gu_own = scattered(dw_gu)

    def norm_back(rows, scale, gain, grad):
        n = rows * scale
        u = grad * gain
        return scale * (u - n * jnp.mean(u * n, axis=-1, keepdims=True))

    middle_grad = cot_own.astype(F32) + norm_back(middle, scale_two, gain_two, normed_two_grad)
    branch = gather_plane(middle_grad.astype(BF))
    dmix = dot_nt(branch, w_out_eff)
    dlin, dmq, dmk = attention_backward(dmix, saved, cos, sin, mq, mk, perm, seq_lengths)
    n1g_away = dot_nt(dlin[half:], w_in_eff).astype(BF)
    n1g_here = dot_nt(dlin[:half], w_in_eff).astype(BF)
    normed_grad = scatter_plane(n1g_away, n1g_here)
    own_wide = rows_in.astype(F32)
    in_own = middle_grad + norm_back(own_wide, scale_of(own_wide), gain_one, normed_grad)
    input_grad = both_tp(in_own.astype(BF)).astype(F32)[None]

    dw_out_t = dot_tn(branch, mixed)
    dw_in = dot_tn(normed, dlin)
    dw_out_low, dw_in_low = dw_out_t.astype(BF), dw_in.astype(BF)
    dw_attn_own = scattered(jnp.concatenate([dw_in_low, dw_out_low], axis=1))

    d_ups = dot(downs, dw_in_low)
    d_out_down = dot(out_up_all, dw_out_low)
    by_shard = lambda a: a.astype(BF).reshape(shards, -1, ds)
    d_qu = d_ups[:rank, :wide].reshape(rank, heads, shards, hs).transpose(2, 0, 1, 3)
    d_ku = d_ups[rank : 2 * rank, wide : wide + 64].reshape(rank, shards, hs).transpose(1, 0, 2)
    d_vu = d_ups[2 * rank :, wide + 64 :].reshape(rank, shards, hs).transpose(1, 0, 2)
    d_both = jnp.concatenate([d_ku.reshape(shards, -1), d_vu.reshape(shards, -1)], axis=1)
    d_od = d_out_down.reshape(rank, heads, shards, hs).transpose(2, 1, 3, 0)
    d_mq = jnp.stack([dmq[h * 64 : (h + 1) * 64, h * 64 : (h + 1) * 64] for h in range(heads)])
    d_mq = d_mq.reshape(heads, shards, hs, 64).transpose(1, 0, 2, 3)
    d_mk = dmk.reshape(shards, hs, 64)
    d_small = jnp.concatenate(
        [
            by_shard(d_mq),
            by_shard(d_mk),
            by_shard(d_qu),
            by_shard(jnp.concatenate([d_both, jnp.zeros_like(d_both)], axis=1)),
            by_shard(d_od),
            jnp.zeros((shards, 3, ds), BF),
        ],
        axis=1,
    )
    d_small_own = lax.psum_scatter(d_small, "shard", scatter_dimension=0, tiled=True)[0]

    dw_in_own = dw_attn_own[:, : wide + 128].astype(F32)
    dw_out_own = dw_attn_own[:, wide + 128 :]
    w_in_eff_own = lax.dynamic_slice_in_dim(w_in_eff, s * ds, ds, 0).astype(F32)
    gain_one_own, gain_two_own = attn_gain.astype(F32), ffn_gain.astype(F32)
    d_gain_one = jnp.sum(w_in_eff_own * dw_in_own, axis=1) / gain_one_own
    d_gain_two = jnp.sum(w_gu_own.astype(F32) * dw_gu_own.astype(F32), axis=1) / gain_two_own
    partial = jnp.concatenate(
        [
            dot_nt(ups, dw_attn_own[:, : wide + 128]),
            lax.dot_general(out_down_all, dw_out_own, (((0,), (1,)), ((), ())), preferred_element_type=F32),
            d_gain_one[None],
            d_gain_two[None],
        ],
        axis=0,
    )
    partial = partial + to_core(partial)
    partial = partial + to_x(partial)
    partial = partial + to_y(partial)

    here = c.astype(jnp.int32)[None]
    gate_grad, up_grad = place(on_ctx(dw_gu_own), here, (units, units))
    (down_grad,) = place(on_ctx(dw_dt_own), here, (), turn=True)
    attn = absolute(on_ctx(dw_attn_own), x, k)
    side = lambda a, b: jnp.concatenate([p[:, a:b] for p in attn], axis=1).astype(F32)
    query_weight_grad = side(0, wide)
    key_weight_grad = side(wide, wide + 64)
    value_weight_grad = side(wide + 64, wide + 128)
    out_weight_grad = side(wide + 128, 2 * wide + 128).T
    smalls = jnp.stack(absolute(on_ctx(d_small_own), x, k)).astype(F32)
    query_map_grad = smalls[:, :8].reshape(4 * heads, hs, 64)
    key_map_grad = smalls[:, 8:10].reshape(4, hs, 64)
    query_up_grad = smalls[:, 10].reshape(4, rank, heads, hs).transpose(1, 0, 2, 3).reshape(rank, 4 * heads, hs)
    both_grad = smalls[:, 11, : ds // 2].reshape(4, 2, rank, hs)
    key_up_grad = both_grad[:, 0].transpose(1, 0, 2)
    value_up_grad = both_grad[:, 1].transpose(1, 0, 2)
    out_down_grad = smalls[:, 12].reshape(4 * heads, hs, rank)
    return (
        outputs,
        input_grad,
        partial[4 * rank],
        query_weight_grad,
        key_weight_grad,
        value_weight_grad,
        out_weight_grad,
        partial[:rank].T,
        query_up_grad,
        partial[rank : 2 * rank].T,
        key_up_grad,
        partial[2 * rank : 3 * rank].T,
        value_up_grad,
        out_down_grad,
        partial[3 * rank : 4 * rank],
        query_map_grad,
        key_map_grad,
        partial[4 * rank + 1],
        gate_grad,
        up_grad,
        down_grad,
    )


def solution(mesh):
    rows = P("shard", "ctx", None)
    in_specs = (
        rows,
        rows,
        P("shard"),
        P("shard"),
        P("shard", "tp"),
        P("shard", "tp"),
        P("shard", "tp"),
        P("tp", "shard"),
        P("shard", None),
        P(None, "tp", "shard"),
        P("shard", None),
        P(None, "tp", "shard"),
        P("shard", None),
        P(None, "tp", "shard"),
        P("tp", "shard", None),
        P(None, "shard"),
        P("tp", "shard", None),
        P("tp", "shard", None),
        P("shard"),
        P("shard", "tp"),
        P("shard", "tp"),
        P("tp", "shard"),
    )
    out_specs = (rows, rows) + in_specs[3:]
    return jax.shard_map(body, mesh=mesh, in_specs=in_specs, out_specs=out_specs, check_vma=False)
```

profile of v0, /device:TPU:0, one launch (start us, length us, event | category | flops | bytes accessed | tf_op | source)
XLA Modules:
  0.0 881.6 jit_solution(18270259303597768815)
XLA Ops:
  26.6 15.7 %all-gather = bf16[192,512]{1,0:T(8,128)(2,1)S(1)} all-gather(bf16[48,512]{1,0:T(8,128)(2,1)S(1)} %concatenate.102), channel_id=2, replica_groups=mesh['shard'=4,'ctx'=4,'tp'=2] {'shard'}, dimensions={0}, use_global_device_ids=true | all-gather | bytes 245760 | tf_op jit(solution)/shard_map/all_gather | solution.py:598
  86.8 9.7 %fusion.21.lin_ref = f32[2048,384]{1,0:T(8,128)} fusion(bf16[2048,384]{0,1:T(8,128)(2,1)S(1)} %add_convert_fusion, bf16[2048,2048]{1,0:T(8,128)(2,1)} %copy-done.27, f32[2048]{0:T(1024)S(1)} %bitcast.324, f32[2048]{0:T(1024)S(1)} %add_rsqrt_fusion), kind=kOutput, calls=%fused_computation.42 | convolution fusion | flops 3238002688 | bytes 13123584 | tf_op jit(solution)/shard_map/dot_general | solution.py:24
  96.5 24.8 %attention_forward.1 = (bf16[2048,256]{1,0:T(8,128)(2,1)S(1)}, f32[2048,256]{1,0:T(8,128)}, f32[2048,256]{1,0:T(8,128)}, bf16[2048,256]{1,0:T(8,128)(2,1)S(1)}, ...) custom-call(s32[8]{0:T(128)S(1)} %xor_add_fusion.perm, ...), custom_call_target="tpu_custom_call" | custom-call | flops 10000000000 | bytes 20971520 | tf_op jit(solution)/shard_map/attention_forward/pallas_call | solution.py:373
  160.5 16.3 %collective-permute-done.32 = bf16[256,2048]{1,0:T(8,128)(2,1)S(1)} collective-permute-done((bf16[256,2048]{1,0:T(8,128)(2,1)}, bf16[256,2048]{1,0:T(8,128)(2,1)S(1)}, u32[]{:S(2)}, u32[]{:S(2)}) %collective-permute-start.32) | collective-permute-done | bytes 1048608 | tf_op jit(solution)/shard_map/ppermute | solution.py:40
  178.6 9.6 %collective-permute-done.9 = bf16[128,2048]{1,0:T(8,128)(2,1)} collective-permute-done((bf16[128,2048]{1,0:T(8,128)(2,1)}, bf16[128,2048]{1,0:T(8,128)(2,1)}, u32[]{:S(2)}, u32[]{:S(2)}) %collective-permute-start.9) | collective-permute-done | bytes 524320 | tf_op jit(solution)/shard_map/ppermute | solution.py:40
  225.3 15.7 %collective-permute-done.15 = bf16[256,2048]{1,0:T(8,128)(2,1)S(1)} collective-permute-done((bf16[256,2048]{1,0:T(8,128)(2,1)S(1)}, bf16[256,2048]{1,0:T(8,128)(2,1)S(1)}, u32[]{:S(2)}, u32[]{:S(2)}) %collective-permute-start.15) | collective-permute-done | bytes 1048608 | tf_op jit(solution)/shard_map/ppermute | solution.py:40
  262.7 24.8 %fusion.95 = f32[2048,2048]{0,1:T(8,128)} fusion(bf16[2048,2048]{1,0:T(8,128)(2,1)} %constant_dynamic-update-slice_fusion.10, bf16[2048,2048]{1,0:T(8,128)(2,1)} %all-gather.9.cloned.1.call-done), kind=kOutput, calls=%fused_computation.278 | convolution fusion | flops 17179869184 | bytes 33554432 | tf_op jit(solution)/shard_map/dot_general | solution.py:24
  287.5 26.4 %all-gather.11.cloned.1.call-done = bf16[2048,1024]{0,1:T(8,128)(2,1)} async-done(((bf16[512,1024]{0,1:T(8,128)(2,1)}), bf16[2048,1024]{0,1:T(8,128)(2,1)}) %all-gather.11.cloned.1.call-update) | async-done | bytes 4194320 | tf_op jit(solution)/shard_map/all_gather | solution.py:568
  313.9 22.2 %multiply_convert_fusion = (bf16[2048,1024]{0,1:T(8,128)(2,1)}, bf16[2048,1024]{0,1:T(8,128)(2,1)}, bf16[2048,1024]{0,1:T(8,128)(2,1)}) fusion(f32[2048,2048]{0,1:T(8,128)} %fusion.95, bf16[2048,2048]{1,0:T(8,128)(2,1)} %constant_dynamic-update-slice_fusion.20, bf16[2048,1024]{0,1:T(8,128)(2,1)} %all-gather.11.cloned.1.call-done), kind=kOutput, calls=%fused_computation.13 | convolution fusion | flops 8621391872 | bytes 41943040 | tf_op jit(solution)/shard_map/dot_general | solution.py:24
  336.1 14.8 %fusion.12 = bf16[1024,2048]{1,0:T(8,128)(2,1)} fusion(bf16[2048,2048]{1,0:T(8,128)(2,1)} %all-gather.9.cloned.1.call-done, bf16[2048,1024]{0,1:T(8,128)(2,1)} %get-tuple-element.168, bf16[2048,1024]{0,1:T(8,128)(2,1)} %get-tuple-element.167), kind=kOutput, calls=%fused_computation.29 | convolution fusion | flops 8600420352 | bytes 20971520 | tf_op jit(solution)/shard_map/dot_general | solution.py:28
  359.2 14.8 %convert_add_fusion.1 = f32[1024,2048]{1,0:T(8,128)} fusion(bf16[1024,2048]{1,0:T(8,128)(2,1)S(1)} %collective-permute-done.40, bf16[2048,2048]{1,0:T(8,128)(2,1)} %all-gather.9.cloned.1.call-done, bf16[2048,1024]{0,1:T(8,128)(2,1)} %get-tuple-element.168, bf16[2048,1024]{0,1:T(8,128)(2,1)} %get-tuple-element.167), kind=kOutput, calls=%fused_computation.12 | convolution fusion | flops 8606711808 | bytes 29360128 | tf_op jit(solution)/shard_map/dot_general | solution.py:28
  380.8 9.2 %convert_add_fusion.2 = f32[1024,2048]{1,0:T(8,128)S(1)} fusion(bf16[1024,2048]{1,0:T(8,128)(2,1)} %collective-permute-done.24, bf16[2048,1024]{0,1:T(8,128)(2,1)} %all-gather.11.cloned.1.call-done, bf16[2048,1024]{0,1:T(8,128)(2,1)} %get-tuple-element.169), kind=kOutput, calls=%fused_computation.15 | convolution fusion | flops 4303355904 | bytes 18874368 | tf_op jit(solution)/shard_map/dot_general | solution.py:28
  432.9 23.4 %collective-permute-done.28 = bf16[128,2048]{1,0:T(8,128)(2,1)S(1)} collective-permute-done((bf16[128,2048]{1,0:T(8,128)(2,1)S(1)}, bf16[128,2048]{1,0:T(8,128)(2,1)S(1)}, u32[]{:S(2)}, u32[]{:S(2)}) %collective-permute-start.28) | collective-permute-done | bytes 524320 | tf_op jit(solution)/shard_map/ppermute | solution.py:44
  456.3 9.7 %collective-permute-done.27 = bf16[128,2048]{1,0:T(8,128)(2,1)S(1)} collective-permute-done((bf16[128,2048]{1,0:T(8,128)(2,1)S(1)}, bf16[128,2048]{1,0:T(8,128)(2,1)S(1)}, u32[]{:S(2)}, u32[]{:S(2)}) %collective-permute-start.27) | collective-permute-done | bytes 524320 | tf_op jit(solution)/shard_map/ppermute | solution.py:44
  467.3 11.5 %collective-permute-done.29 = bf16[128,2048]{1,0:T(8,128)(2,1)S(1)} collective-permute-done((bf16[128,2048]{1,0:T(8,128)(2,1)S(1)}, bf16[128,2048]{1,0:T(8,128)(2,1)S(1)}, u32[]{:S(2)}, u32[]{:S(2)}) %collective-permute-start.29) | collective-permute-done | bytes 524320 | tf_op jit(solution)/shard_map/ppermute | solution.py:40
  486.9 11.0 %convolution_convert_fusion.3 = bf16[2048,1024]{1,0:T(8,128)(2,1)} fusion(bf16[2048,2048]{1,0:T(8,128)(2,1)S(1)} %bitcast.319, bf16[2048,1024]{0,1:T(8,128)(2,1)S(1)} %copy-done.78), kind=kOutput, calls=%fused_computation.30 | convolution fusion | flops 8592031744 | bytes 16777216 | tf_op jit(solution)/shard_map/dot_general | solution.py:32
  498.1 10.0 %collective-permute-done.47 = bf16[256,2048]{1,0:T(8,128)(2,1)} collective-permute-done((bf16[256,2048]{1,0:T(8,128)(2,1)}, bf16[256,2048]{1,0:T(8,128)(2,1)}, u32[]{:S(2)}, u32[]{:S(2)}) %collective-permute-start.47) | collective-permute-done | bytes 1048608 | tf_op jit(solution)/shard_map/ppermute | solution.py:40
  535.1 27.9 %attention_backward.1 = (bf16[2048,384]{1,0:T(8,128)(2,1)}, f32[256,256]{1,0:T(8,128)S(1)}, f32[64,64]{1,0:T(8,128)S(1)}) custom-call(s32[8]{0:T(128)S(1)} %copy-done.9, s32[1]{0:T(128)} %copy.171.length, f32[2048,256]{1,0:T(8,128)} %fusion.96.dmix_ref, f32[2048,256]{1,0:T(8,128)} %get-tuple-element.73.mix_ref, f32[2048,256]{1,0:T(8,128)} %get-tuple-element.74.rden_ref, ...), custom_call_target="tpu_custom_call" | custom-call | flops 20000000000 | bytes 20971520 | tf_op jit(solution)/shard_map/attention_backward/pallas_call | solution.py:444
  585.4 23.9 %fusion.5 = bf16[2048,2048]{1,0:T(8,128)(2,1)} fusion(bf16[2048,2048]{1,0:T(8,128)(2,1)} %constant_dynamic-update-slice_fusion.10, bf16[2048,1024]{0,1:T(8,128)(2,1)} %get-tuple-element.167, bf16[2048,1024]{0,1:T(8,128)(2,1)} %get-tuple-element.168), kind=kOutput, calls=%fused_computation.20 | convolution fusion | flops 17200840704 | bytes 25165824 | tf_op jit(solution)/shard_map/dot_general | solution.py:32
  664.6 10.0 %place.3 = f32[4096,512]{1,0:T(8,128)} custom-call(s32[1]{0:T(128)} %bitcast.98.at, bf16[512,1024]{1,0:T(8,128)(2,1)S(1)} %copy-done.5, bf16[512,1024]{1,0:T(8,128)(2,1)S(1)} %collective-permute-done.76.refs_1_, bf16[512,1024]{1,0:T(8,128)(2,1)S(1)} %collective-permute-done.77.refs_2_, bf16[512,1024]{1,0:T(8,128)(2,1)} %collective-permute-done.78.refs_3_), custom_call_target="tpu_custom_call" | custom-call | tf_op jit(solution)/shard_map/place/pallas_call | solution.py:489
  703.8 9.4 %collective-permute-done.67 = bf16[512,640]{0,1:T(8,128)(2,1)S(1)} collective-permute-done((bf16[512,640]{0,1:T(8,128)(2,1)}, bf16[512,640]{0,1:T(8,128)(2,1)S(1)}, u32[]{:S(2)}, u32[]{:S(2)}) %collective-permute-start.67) | collective-permute-done | bytes 655392 | tf_op jit(solution)/shard_map/ppermute | solution.py:40
  716.5 82.1 %reduce-scatter.7.cloned.1.call-done.refs_0_ = bf16[512,2048]{1,0:T(8,128)(2,1)} async-done(((bf16[2048,2048]{1,0:T(8,128)(2,1)}), bf16[512,2048]{1,0:T(8,128)(2,1)}) %reduce-scatter.7.cloned.1.call-update) | async-done | bytes 2097168 | tf_op jit(solution)/shard_map/reduce_scatter | solution.py:685
  812.9 33.2 %collective-permute-done.74.refs_2_ = bf16[512,2048]{1,0:T(8,128)(2,1)} collective-permute-done((bf16[512,2048]{1,0:T(8,128)(2,1)}, bf16[512,2048]{1,0:T(8,128)(2,1)}, u32[]{:S(2)}, u32[]{:S(2)}) %collective-permute-start.74) | collective-permute-done | bytes 2097184 | tf_op jit(solution)/shard_map/ppermute | solution.py:40
  860.7 13.6 %place.2 = (f32[512,4096]{1,0:T(8,128)}, f32[512,4096]{1,0:T(8,128)}) custom-call(s32[1]{0:T(128)} %bitcast.98.at, bf16[512,2048]{1,0:T(8,128)(2,1)S(1)} %copy-done.2, bf16[512,2048]{1,0:T(8,128)(2,1)} %collective-permute-done.73.refs_1_, bf16[512,2048]{1,0:T(8,128)(2,1)} %collective-permute-done.74.refs_2_, bf16[512,2048]{1,0:T(8,128)(2,1)} %collective-permute-done.75.refs_3_), custom_call_target="tpu_custom_call" | custom-call | tf_op jit(solution)/shard_map/place/pallas_call | solution.py:489
  (562 shorter events, 395.2 us)
Async XLA Ops:
  7.2 65.7 %all-gather.13.cloned.1.call-start = ((), (), s32[]{:S(2)}) async-start(), calls=%async_computation.11 | async-start | bytes 1310720 | tf_op jit(solution)/shard_map/all_gather | solution.py:616
  9.2 74.4 %all-gather.7.cloned.1.call-start = ((), (), s32[]{:S(2)}) async-start(), calls=%async_computation.4 | async-start | bytes 1966080 | tf_op jit(solution)/shard_map/all_gather | solution.py:568
  12.5 250.2 %all-gather.9.cloned.1.call-start = ((), (), s32[]{:S(2)}) async-start(), calls=%async_computation.5 | async-start | bytes 10485760 | tf_op jit(solution)/shard_map/all_gather | solution.py:568
  13.8 37.4 %collective-permute-start = (bf16[256,2048]{1,0:T(8,128)(2,1)S(1)}, bf16[256,2048]{1,0:T(8,128)(2,1)}, u32[]{:S(2)}, u32[]{:S(2)}) collective-permute-start(bf16[256,2048]{1,0:T(8,128)(2,1)S(1)} %get-tuple-element.166), channel_id=1, source_target_pairs={{0,4},{2,6},{4,0},{6,2},{1,5},{3,7},{5,1},{7,3},{8,12},{10,14},{12... | collective-permute-start | bytes 3145736 | tf_op jit(solution)/shard_map/ppermute | solution.py:40
  16.7 53.9 %collective-permute-start.3 = (bf16[256,2048]{1,0:T(8,128)(2,1)S(1)}, bf16[256,2048]{1,0:T(8,128)(2,1)}, u32[]{:S(2)}, u32[]{:S(2)}) collective-permute-start(bf16[256,2048]{1,0:T(8,128)(2,1)S(1)} %get-tuple-element.166), channel_id=1, source_target_pairs={{0,2},{2,0},{4,6},{6,4},{1,3},{3,1},{5,7},{7,5},{8,10},{10,8},{12,... | collective-permute-start | bytes 3145736 | tf_op jit(solution)/shard_map/ppermute | solution.py:36
  22.2 291.7 %all-gather.11.cloned.1.call-start = ((), (), s32[]{:S(2)}) async-start(), calls=%async_computation.6 | async-start | bytes 5242880 | tf_op jit(solution)/shard_map/all_gather | solution.py:568
  145.3 42.9 %collective-permute-start.9 = (bf16[128,2048]{1,0:T(8,128)(2,1)}, bf16[128,2048]{1,0:T(8,128)(2,1)}, u32[]{:S(2)}, u32[]{:S(2)}) collective-permute-start(bf16[128,2048]{1,0:T(8,128)(2,1)} %get-tuple-element.190), channel_id=1, source_target_pairs={{0,4},{2,6},{4,0},{6,2},{1,5},{3,7},{5,1},{7,3},{8,12},{10,14},{12... | collective-permute-start | bytes 1572872 | tf_op jit(solution)/shard_map/ppermute | solution.py:40
  145.6 44.3 %collective-permute-start.12 = (bf16[128,2048]{1,0:T(8,128)(2,1)}, bf16[128,2048]{1,0:T(8,128)(2,1)}, u32[]{:S(2)}, u32[]{:S(2)}) collective-permute-start(bf16[128,2048]{1,0:T(8,128)(2,1)} %get-tuple-element.192), channel_id=1, source_target_pairs={{0,1},{1,0},{2,3},{3,2},{4,5},{5,4},{6,7},{7,6},{8,9},{9,8},{10,11... | collective-permute-start | bytes 1572872 | tf_op jit(solution)/shard_map/ppermute | solution.py:44
  155.2 34.9 %collective-permute-start.11 = (bf16[128,2048]{1,0:T(8,128)(2,1)}, bf16[128,2048]{1,0:T(8,128)(2,1)}, u32[]{:S(2)}, u32[]{:S(2)}) collective-permute-start(bf16[128,2048]{1,0:T(8,128)(2,1)} %fusion.62), channel_id=1, source_target_pairs={{0,1},{1,0},{2,3},{3,2},{4,5},{5,4},{6,7},{7,6},{8,9},{9,8},{10,11... | collective-permute-start | bytes 1572872 | tf_op jit(solution)/shard_map/ppermute | solution.py:44
  157.0 62.6 %collective-permute-start.35 = (bf16[256,2048]{1,0:T(8,128)(2,1)}, bf16[256,2048]{1,0:T(8,128)(2,1)}, u32[]{:S(2)}, u32[]{:S(2)}) collective-permute-start(bf16[256,2048]{1,0:T(8,128)(2,1)} %get-tuple-element.160), channel_id=1, source_target_pairs={{0,2},{2,0},{4,6},{6,4},{1,3},{3,1},{5,7},{7,5},{8,10},{10,8},{12,... | collective-permute-start | bytes 3145736 | tf_op jit(solution)/shard_map/ppermute | solution.py:36
  159.3 458.1 %reduce-scatter.11.cloned.1.call-start = ((), (), s32[]{:S(2)}) async-start(), calls=%async_computation.10 | async-start | bytes 5242880 | tf_op jit(solution)/shard_map/reduce_scatter | solution.py:685
  176.8 40.4 %collective-permute-start.34 = (bf16[128,2048]{1,0:T(8,128)(2,1)S(1)}, bf16[128,2048]{1,0:T(8,128)(2,1)S(1)}, u32[]{:S(2)}, u32[]{:S(2)}) collective-permute-start(bf16[128,2048]{1,0:T(8,128)(2,1)S(1)} %constant_dynamic-slice_fusion), channel_id=1, source_target_pairs={{0,4},{2,6},{4,0},{6,2},{1,5},{3,7},{5,1},{7,3},{8,12},{10,14},{12... | collective-permute-start | bytes 1572872 | tf_op jit(solution)/shard_map/ppermute | solution.py:40
  398.7 68.4 %collective-permute-start.46 = (bf16[128,2048]{1,0:T(8,128)(2,1)}, bf16[128,2048]{1,0:T(8,128)(2,1)S(1)}, u32[]{:S(2)}, u32[]{:S(2)}) collective-permute-start(bf16[128,2048]{1,0:T(8,128)(2,1)} %get-tuple-element.183), channel_id=1, source_target_pairs={{0,1},{1,0},{2,3},{3,2},{4,5},{5,4},{6,7},{7,6},{8,9},{9,8},{10,11... | collective-permute-start | bytes 1572872 | tf_op jit(solution)/shard_map/ppermute | solution.py:44
  409.2 58.1 %collective-permute-start.30 = (bf16[128,2048]{1,0:T(8,128)(2,1)S(1)}, bf16[128,2048]{1,0:T(8,128)(2,1)S(1)}, u32[]{:S(2)}, u32[]{:S(2)}) collective-permute-start(bf16[128,2048]{1,0:T(8,128)(2,1)S(1)} %get-tuple-element.187), channel_id=1, source_target_pairs={{0,1},{1,0},{2,3},{3,2},{4,5},{5,4},{6,7},{7,6},{8,9},{9,8},{10,11... | collective-permute-start | bytes 1572872 | tf_op jit(solution)/shard_map/ppermute | solution.py:44
  420.2 36.1 %collective-permute-start.28 = (bf16[128,2048]{1,0:T(8,128)(2,1)S(1)}, bf16[128,2048]{1,0:T(8,128)(2,1)S(1)}, u32[]{:S(2)}, u32[]{:S(2)}) collective-permute-start(bf16[128,2048]{1,0:T(8,128)(2,1)S(1)} %get-tuple-element.188), channel_id=1, source_target_pairs={{0,1},{1,0},{2,3},{3,2},{4,5},{5,4},{6,7},{7,6},{8,9},{9,8},{10,11... | collective-permute-start | bytes 1572872 | tf_op jit(solution)/shard_map/ppermute | solution.py:44
  422.6 43.4 %collective-permute-start.27 = (bf16[128,2048]{1,0:T(8,128)(2,1)S(1)}, bf16[128,2048]{1,0:T(8,128)(2,1)S(1)}, u32[]{:S(2)}, u32[]{:S(2)}) collective-permute-start(bf16[128,2048]{1,0:T(8,128)(2,1)S(1)} %fusion.54), channel_id=1, source_target_pairs={{0,1},{1,0},{2,3},{3,2},{4,5},{5,4},{6,7},{7,6},{8,9},{9,8},{10,11... | collective-permute-start | bytes 1572872 | tf_op jit(solution)/shard_map/ppermute | solution.py:44
  432.5 34.6 %collective-permute-start.45 = (bf16[128,2048]{1,0:T(8,128)(2,1)S(1)}, bf16[128,2048]{1,0:T(8,128)(2,1)S(1)}, u32[]{:S(2)}, u32[]{:S(2)}) collective-permute-start(bf16[128,2048]{1,0:T(8,128)(2,1)S(1)} %get-tuple-element.173), channel_id=1, source_target_pairs={{0,4},{2,6},{4,0},{6,2},{1,5},{3,7},{5,1},{7,3},{8,12},{10,14},{12... | collective-permute-start | bytes 1572872 | tf_op jit(solution)/shard_map/ppermute | solution.py:40
  497.9 146.6 %reduce-scatter.9.cloned.1.call-start = ((), (), s32[]{:S(2)}) async-start(), calls=%async_computation.9 | async-start | bytes 81920 | tf_op jit(solution)/shard_map/reduce_scatter | solution.py:733
  582.3 105.4 %reduce-scatter.5.cloned.1.call-start = ((), (), s32[]{:S(2)}) async-start(), calls=%async_computation.7 | async-start | bytes 3276800 | tf_op jit(solution)/shard_map/reduce_scatter | solution.py:685
  585.4 213.2 %reduce-scatter.7.cloned.1.call-start = ((), (), s32[]{:S(2)}) async-start(), calls=%async_computation.8 | async-start | bytes 10485760 | tf_op jit(solution)/shard_map/reduce_scatter | solution.py:685
  617.3 37.2 %collective-permute-start.77 = (bf16[512,1024]{1,0:T(8,128)(2,1)}, bf16[512,1024]{1,0:T(8,128)(2,1)S(1)}, u32[]{:S(2)}, u32[]{:S(2)}) collective-permute-start(bf16[512,1024]{1,0:T(8,128)(2,1)} %reduce-scatter.11.cloned.1.call-done.refs_0_), channel_id=1, source_target_pairs={{0,4},{2,6},{4,0},{6,2},{1,5},{3,7},{5,1},{7,3},{8,12},{10,14},{12... | collective-permute-start | bytes 3145736 | tf_op jit(solution)/shard_map/ppermute | solution.py:40
  714.8 137.1 %collective-permute-start.63 = (bf16[256,2048]{1,0:T(8,128)(2,1)}, bf16[256,2048]{1,0:T(8,128)(2,1)}, u32[]{:S(2)}, u32[]{:S(2)}) collective-permute-start(bf16[256,2048]{1,0:T(8,128)(2,1)} %fusion.27), channel_id=1, source_target_pairs={{0,1},{1,0},{2,3},{3,2},{4,5},{5,4},{6,7},{7,6},{8,9},{9,8},{10,11... | collective-permute-start | bytes 3145736 | tf_op jit(solution)/shard_map/ppermute | solution.py:44
  798.6 47.5 %collective-permute-start.74 = (bf16[512,2048]{1,0:T(8,128)(2,1)}, bf16[512,2048]{1,0:T(8,128)(2,1)}, u32[]{:S(2)}, u32[]{:S(2)}) collective-permute-start(bf16[512,2048]{1,0:T(8,128)(2,1)} %reduce-scatter.7.cloned.1.call-done.refs_0_), channel_id=1, source_target_pairs={{0,4},{2,6},{4,0},{6,2},{1,5},{3,7},{5,1},{7,3},{8,12},{10,14},{12... | collective-permute-start | bytes 6291464 | tf_op jit(solution)/shard_map/ppermute | solution.py:40
  812.9 47.8 %collective-permute-start.73 = (bf16[512,2048]{1,0:T(8,128)(2,1)S(1)}, bf16[512,2048]{1,0:T(8,128)(2,1)}, u32[]{:S(2)}, u32[]{:S(2)}) collective-permute-start(bf16[512,2048]{1,0:T(8,128)(2,1)S(1)} %copy-done.2), channel_id=1, source_target_pairs={{0,2},{2,0},{4,6},{6,4},{1,3},{3,1},{5,7},{7,5},{8,10},{10,8},{12,... | collective-permute-start | bytes 6291464 | tf_op jit(solution)/shard_map/ppermute | solution.py:36
  (146 other events, 2423.1 us)
Sparse Core Ops, SparseCore 0:
  10.2 33.7 all-gather.12
  46.2 36.5 all-gather.6
  84.9 148.4 all-gather.8
  234.9 78.9 all-gather.10
  498.1 74.4 reduce-scatter.10
  582.4 16.4 reduce-scatter.8
  601.2 50.2 reduce-scatter.4
  654.4 144.1 reduce-scatter.6
where the time goes:
time: 893 us; the launch traced here: 882 us
  waiting for transfers between devices  370 us (41%)
  matrix products  185 us (21%)
  local copies, waits for them, and re-layouts  102 us (11%)
  Pallas kernels  76.3 us (9%)
  starting transfers between devices  59.5 us (7%)
  other arithmetic  57 us (6%)
  between operations  16.8 us (2%)
  blocking collectives  15.7 us (2%)
    ppermute x25, waiting for transfers between devices, to_x(): return lax.ppermute(a, 'ctx', ALONG_X)  159 us
    ppermute x21, waiting for transfers between devices, to_y(): return lax.ppermute(a, 'tp', ALONG_Y)  88.7 us
    reduce_scatter x3, waiting for transfers between devices, scattered(): return lax.psum_scatter(a, 'shard', scatter_dimension=0, tiled=True)  82.1 us
    dot_general x8, matrix products, dot(): return jnp.dot(a, b, preferred_element_type=F32)  67.2 us
    dot_general x8, matrix products, dot_nt(): lax.dot_general(a, b, (((1,), (1,)), ((), ())), preferred_element_type=F32)  65.9 us
    unnamed x212, local copies, waits for them, and re-layouts  62.2 us
    dot_general x5, matrix products, dot_tn(): lax.dot_general(a, b, (((0,), (0,)), ((), ())), preferred_element_type=F32)  50.6 us
    pallas_call x1, Pallas kernels, attention_backward(): pl.pallas_call(functools.partial(backward_kernel, heads), grid_spec=grid,...  27.9 us
  transfers between devices with their start and end apart: 87, of which 34 were waited for; matrix products, arithmetic and copies ran while one was open for 33% of the time, Pallas kernels for 7%

commit v1 on v0

--- a/solution.py
+++ b/solution.py
@@ -5,6 +5,7 @@
 import numpy as np
 from jax import lax
 from jax.experimental import pallas as pl
+from jax.experimental.layout import Layout, with_layout_constraint
 from jax.experimental.pallas import tpu as pltpu
 from jax.sharding import PartitionSpec as P
 
@@ -14,6 +15,7 @@
 SCALE = 0.125
 BF = jnp.bfloat16
 F32 = jnp.float32
+LITTLE = pl.CostEstimate(flops=1 << 20, bytes_accessed=1 << 16, transcendentals=0)
 
 CORE = [(c, c ^ 1) for c in range(4)]
 ALONG_X = [(c, c ^ 2) for c in range(4)]
@@ -44,34 +46,70 @@
     return lax.ppermute(a, "tp", ALONG_Y)
 
 
-def gather_plane(own, y_piece=None):
+def gather_plane(own, y_piece=None, later=()):
     half = own.shape[0] // 2
     px = to_x(own)
     py = to_y(own) if y_piece is None else y_piece
     c0 = to_core(own)
-    bxy = to_x(py[half:])
+    if y_piece is not None:
+        bxy = to_x(py[half:])
+    if callable(later):
+        later = later(c0)
+    if later:
+        px, py = after(px, *later), after(py, *later)
+    if y_piece is None:
+        bxy = to_x(py[half:])
     axy = to_y(px[:half])
     cx, cy = to_core(px), to_core(py)
     caxy, cbxy = to_core(axy), to_core(bxy)
-    return jnp.concatenate([own, px, py, axy, bxy, c0, cx, cy, caxy, cbxy], axis=0)
-
-
-def scatter_plane(away, here):
-    rows, n = here.shape[0] // 4, here.shape[1]
-    got = to_core(away)
-    s = (here.astype(F32) + got.astype(F32)).reshape(4, 2, rows // 2, n)
-    low = s.astype(BF)
-    r3a, r3b = to_x(low[3, 0]), to_y(low[3, 1])
-    r1a, r2b = to_x(low[1, 0]), to_y(low[2, 1])
-    r1b = to_x((s[1, 1] + r3b.astype(F32)).astype(BF))
-    r2a = to_y((s[2, 0] + r3a.astype(F32)).astype(BF))
-    return jnp.concatenate(
-        [
-            s[0, 0] + r1a.astype(F32) + r2a.astype(F32),
-            s[0, 1] + r1b.astype(F32) + r2b.astype(F32),
-        ],
-        axis=0,
-    )
+    return [own, px, py, axy, bxy, c0, cx, cy, caxy, cbxy], (axy, bxy)
+
+
+class Scatter:
+    def __init__(self, away, here, *later):
+        self.rows = here.shape[0] // 4
+        self.got = to_core(away)
+        self.here = after(here, *later) if later else here
+        sides = ((3, 0), (3, 1), (1, 0), (2, 1))
+        self.first = lax.optimization_barrier(tuple(self.at(*s).astype(BF) for s in sides))
+
+    def at(self, piece, side, *more):
+        half = self.rows // 2
+        r = slice(piece * self.rows + side * half, piece * self.rows + (side + 1) * half)
+        total = self.here[r].astype(F32) + self.got[r].astype(F32)
+        for m in more:
+            total = total + m.astype(F32)
+        return total
+
+    def step(self):
+        r3a, r3b = to_x(self.first[0]), to_y(self.first[1])
+        self.r1a, self.r2b = to_x(self.first[2]), to_y(self.first[3])
+        self.second = lax.optimization_barrier(
+            (self.at(1, 1, r3b).astype(BF), self.at(2, 0, r3a).astype(BF))
+        )
+        return self
+
+    def last(self):
+        self.r1b, self.r2a = to_x(self.second[0]), to_y(self.second[1])
+        return self
+
+    def own(self):
+        return jnp.concatenate([self.at(0, 0, self.r1a, self.r2a), self.at(0, 1, self.r1b, self.r2b)], axis=0)
+
+
+def scatter_shards(a, shards):
+    if shards > 4:
+        return lax.psum_scatter(a, "shard", scatter_dimension=0, tiled=True)[0].astype(F32)
+    s = lax.axis_index("shard")
+    total = lax.dynamic_index_in_dim(a, s, 0, keepdims=False).astype(F32)
+    for far in range(1, shards):
+        sent = lax.dynamic_index_in_dim(a, (s + far) % shards, 0, keepdims=False)
+        total = total + lax.ppermute(sent, "shard", [(i, (i + far) % shards) for i in range(shards)]).astype(F32)
+    return total
+
+
+def after(a, *others):
+    return lax.optimization_barrier((a, *others))[0]
 
 
 def stack(m, heads):
@@ -218,9 +256,15 @@
 
 def backward_kernel(
     heads,
-    perm,
+    table,
     length,
-    dmix_ref,
+    *refs,
+):
+    pieces, refs = refs[:10], refs[10:]
+    (w_ref,
+    low_ref,
+    normed_ref,
+    mixed_ref,
     mix_ref,
     rden_ref,
     q_ref,
@@ -236,26 +280,46 @@
     sin_ref,
     mq_ref,
     mk_ref,
-    dlin_ref,
+    away_ref,
+    here_ref,
+    dw_ref,
+    dlow_ref,
     dmq_ref,
     dmk_ref,
+    branch_ref,
+    dlin_ref,
+    acc,
     carry,
     carry_f,
     rt,
     rn,
+    dmix_ref,
     dq_s,
     dql_s,
     dkv_s,
-    df_s,
-):
+    df_s) = refs
     g = pl.program_id(0)
     i = pl.num_programs(0) - 1 - g
     rows = dmix_ref.shape[0]
+    half = rows // 2
     blocks = rows // BLOCK
     wide = heads * 64
+    r_here = table[i]
+    for n, held in enumerate(((0,), (1,), (2,), (3, 4), (5,), (6,), (7,), (8, 9))):
+
+        @pl.when(r_here == n)
+        def _(held=held):
+            if len(held) == 1:
+                branch_ref[...] = pieces[held[0]][...]
+            else:
+                branch_ref[:half, :] = pieces[held[0]][...]
+                branch_ref[half:, :] = pieces[held[1]][...]
+
+    dmix_ref[...] = dot(branch_ref[...], w_ref[:, wide + 128 :])
 
     @pl.when(g == 0)
     def _():
+        acc[...] = jnp.zeros_like(acc)
         carry[...] = jnp.zeros_like(carry)
         carry_f[...] = jnp.zeros_like(carry_f)
         rt[...] = jnp.zeros_like(rt)
@@ -327,6 +391,26 @@
     dk_map = dot_nt(dkl, mk_ref[...])
     dkv = dkv_s[...] + jnp.concatenate([dk_map, jnp.zeros_like(dk_map)], axis=1)
     dlin_ref[:, wide:] = turned(dkv, *key_tables(cos, sin)).astype(BF)
+    n1g = dot_nt(dlin_ref[...], w_ref[:, : wide + 128]).astype(BF)
+
+    @pl.when(r_here >= 4)
+    def _():
+        away_ref[...] = n1g
+
+    @pl.when(r_here < 4)
+    def _():
+        here_ref[...] = n1g
+
+    acc[: wide + 128, :] += dot_tn(dlin_ref[...], normed_ref[...])
+    acc[wide + 128 :, :] += dot_tn(mixed_ref[...], branch_ref[...])
+
+    @pl.when(i == 0)
+    def _():
+        low = acc[...].astype(BF)
+        ds = dw_ref.shape[2]
+        for n in range(dw_ref.shape[0]):
+            dw_ref[n] = low[:, n * ds : (n + 1) * ds]
+        dlow_ref[...] = dot_nt(low_ref[...], low)
 
 
 def attention_forward(lin, cos, sin, mq, mk, perm, seq_lengths):
@@ -386,28 +470,37 @@
             made(pieces, 8, 128, F32),
         ],
         compiler_params=pltpu.CompilerParams(vmem_limit_bytes=48 << 20),
-        cost_estimate=pl.CostEstimate(flops=10**10, bytes_accessed=20 << 20, transcendentals=1 << 22),
+        cost_estimate=LITTLE,
         name="attention_forward",
     )(perm, seq_lengths, lin, cos, sin, mq, mk)
 
 
-def attention_backward(dmix, saved, cos, sin, mq, mk, perm, seq_lengths):
+def attention_backward(branch_pieces, w_eff, low_in, normed, mixed, shards, saved, cos, sin, mq, mk, perm, k, seq_lengths):
     mix, rden, q, kv, qf, kf, a, st, norm = saved
-    slots, wide = dmix.shape
+    slots, wide = mix.shape
+    width = w_eff.shape[0]
     heads = wide // 64
     pieces = perm.shape[0]
     rows = slots // pieces
     blocks = rows // BLOCK
     span = heads * rows
     last = pieces - 1
-    moved = lambda g, perm, length: (perm[last - g], 0)
-    plain = lambda g, perm, length: (last - g, 0)
-    prior = lambda g, perm, length: (jnp.maximum((last - g) * blocks - 1, 0), 0)
-    fixed = lambda g, perm, length: (0, 0)
+    back = perm[::-1] & 3
+    one, two = back[np.array([0, 1, 1, 1, 4, 5, 5, 5])], back[np.array([2, 2, 2, 3, 3, 3, 6, 7])]
+    table = jnp.concatenate([perm, jnp.where(k == 0, one, two), jnp.where(k == 0, two, one)])
+    moved = lambda g, table, length: (table[last - g], 0)
+    plain = lambda g, table, length: (last - g, 0)
+    prior = lambda g, table, length: (jnp.maximum((last - g) * blocks - 1, 0), 0)
+    fixed = lambda g, table, length: (0, 0)
+    once = lambda a: pl.BlockSpec(a.shape, fixed, pipeline_mode=pl.Buffered(1))
     grid = pltpu.PrefetchScalarGridSpec(
         num_scalar_prefetch=2,
         grid=(pieces,),
-        in_specs=[
+        in_specs=[once(p) for p in branch_pieces]
+        + [
+            once(w_eff),
+            once(low_in),
+            pl.BlockSpec((rows, width), moved),
             pl.BlockSpec((rows, wide), moved),
             pl.BlockSpec((rows, wide), plain),
             pl.BlockSpec((rows, wide), plain),
@@ -419,84 +512,213 @@
             pl.BlockSpec((BLOCK, 128), prior),
             pl.BlockSpec((span, 128), plain),
             pl.BlockSpec((rows, 128), plain),
-            pl.BlockSpec((1, 8, 128), lambda g, perm, length: (last - g, 0, 0)),
+            pl.BlockSpec((1, 8, 128), lambda g, table, length: (last - g, 0, 0)),
             pl.BlockSpec((rows, 128), plain),
             pl.BlockSpec((rows, 128), plain),
             pl.BlockSpec((wide, wide), fixed),
             pl.BlockSpec((64, 64), fixed),
         ],
         out_specs=[
-            pl.BlockSpec((rows, wide + 128), moved),
+            pl.BlockSpec((rows, width), lambda g, table, length: (table[pieces + g], 0)),
+            pl.BlockSpec((rows, width), lambda g, table, length: (table[2 * pieces + g], 0)),
+            pl.BlockSpec(
+                (shards, w_eff.shape[1], width // shards),
+                lambda g, table, length: (0, 0, 0),
+                pipeline_mode=pl.Buffered(1),
+            ),
+            pl.BlockSpec((low_in.shape[0], w_eff.shape[1]), fixed),
             pl.BlockSpec((wide, wide), fixed),
             pl.BlockSpec((64, 64), fixed),
         ],
         scratch_shapes=[
+            pltpu.VMEM((rows, width), BF),
+            pltpu.VMEM((rows, wide + 128), BF),
+            pltpu.VMEM((w_eff.shape[1], width), F32),
             pltpu.VMEM((BLOCK, 128), F32),
             pltpu.VMEM((BLOCK, 128), F32),
             pltpu.VMEM((64, 128), F32),
             pltpu.VMEM((1, 128), F32),
             pltpu.VMEM((rows, wide), F32),
+            pltpu.VMEM((rows, wide), F32),
             pltpu.VMEM((rows, wide), BF),
             pltpu.VMEM((rows, 128), F32),
             pltpu.VMEM((rows, 128), F32),
         ],
     )
+    made = lambda *s: jax.ShapeDtypeStruct(s[:-1], s[-1])
     return pl.pallas_call(
         functools.partial(backward_kernel, heads),
         grid_spec=grid,
         out_shape=[
-            jax.ShapeDtypeStruct((slots, wide + 128), BF),
-            jax.ShapeDtypeStruct((wide, wide), F32),
-            jax.ShapeDtypeStruct((64, 64), F32),
+            made(slots // 2, width, BF),
+            made(slots // 2, width, BF),
+            made(shards, w_eff.shape[1], width // shards, BF),
+            made(low_in.shape[0], w_eff.shape[1], F32),
+            made(wide, wide, F32),
+            made(64, 64, F32),
         ],
         compiler_params=pltpu.CompilerParams(vmem_limit_bytes=48 << 20),
-        cost_estimate=pl.CostEstimate(flops=2 * 10**10, bytes_accessed=20 << 20, transcendentals=0),
+        cost_estimate=pl.CostEstimate(flops=2 * 10**10, bytes_accessed=16 << 20, transcendentals=0),
         name="attention_backward",
-    )(perm, seq_lengths, dmix, mix, rden, q, kv, kv, qf, kf, kf, a, st, norm, cos, sin, mq, mk)
+    )(table, seq_lengths, *branch_pieces, w_eff, low_in, normed, mixed, mix, rden, q, kv, kv, qf, kf, kf, a, st, norm, cos, sin, mq, mk)
+
+
+def units_kernel(h_ref, w_ref, active_ref, silu_ref, slope_ref):
+    units = active_ref.shape[1]
+    h = h_ref[...]
+    gate = dot(h, w_ref[:, :units])
+    up = dot(h, w_ref[:, units:])
+    sig = 1.0 / (1.0 + jnp.exp(-gate))
+    silu = gate * sig
+    active_ref[...] = (silu * up).astype(BF)
+    silu_ref[...] = silu.astype(BF)
+    slope_ref[...] = (up * (sig + silu * (1.0 - sig))).astype(BF)
+
+
+def hidden_units(h, w_gu):
+    rows, width = h.shape
+    units = w_gu.shape[1] // 2
+    tile = rows // 8
+    return pl.pallas_call(
+        units_kernel,
+        grid=(8,),
+        in_specs=[
+            pl.BlockSpec((tile, width), lambda i: (i, 0)),
+            pl.BlockSpec((width, 2 * units), lambda i: (0, 0), pipeline_mode=pl.Buffered(1)),
+        ],
+        out_specs=[pl.BlockSpec((tile, units), lambda i: (i, 0))] * 3,
+        out_shape=[jax.ShapeDtypeStruct((rows, units), BF)] * 3,
+        compiler_params=pltpu.CompilerParams(vmem_limit_bytes=40 << 20),
+        cost_estimate=LITTLE,
+        name="hidden_units",
+    )(h, w_gu)
+
+
+def units_back_kernel(cot_ref, silu_ref, slope_ref, w_dt_ref, w_gu_ref, *refs):
+    grad_ref, n2g_ref = refs[-2:]
+    units = silu_ref.shape[1]
+    active_grad = dot(cot_ref[...], w_dt_ref[...])
+    grad_ref[:, :units] = (active_grad * slope_ref[...].astype(F32)).astype(BF)
+    grad_ref[:, units:] = (active_grad * silu_ref[...].astype(F32)).astype(BF)
+    n2g_ref[...] = dot_nt(grad_ref[...], w_gu_ref[...]).astype(BF)
+
+
+def hidden_units_back(cot, silu, slope, w_dt, w_gu, second, grads=None):
+    rows, width = cot.shape
+    units = silu.shape[1]
+    steps = 4
+    tile = rows // 2 // steps
+    first = steps if second else 0
+    at = lambda i: (i + first, 0)
+    fixed = lambda i: (0, 0)
+    in_specs = [
+        pl.BlockSpec((tile, width), at),
+        pl.BlockSpec((tile, units), at),
+        pl.BlockSpec((tile, units), at),
+        pl.BlockSpec((width, units), fixed, pipeline_mode=pl.Buffered(1)),
+        pl.BlockSpec((width, 2 * units), fixed, pipeline_mode=pl.Buffered(1)),
+    ]
+    operands = [cot, silu, slope, w_dt, w_gu]
+    if grads is not None:
+        in_specs.append(pl.BlockSpec(memory_space=pl.ANY))
+        operands.append(grads)
+    return pl.pallas_call(
+        units_back_kernel,
+        grid=(steps,),
+        in_specs=in_specs,
+        out_specs=[
+            pl.BlockSpec((tile, 2 * units), at),
+            pl.BlockSpec((tile, width), lambda i: (i, 0)),
+        ],
+        out_shape=[
+            jax.ShapeDtypeStruct((rows, 2 * units), BF),
+            jax.ShapeDtypeStruct((rows // 2, width), BF),
+        ],
+        input_output_aliases={} if grads is None else {5: 0},
+        compiler_params=pltpu.CompilerParams(vmem_limit_bytes=44 << 20),
+        cost_estimate=LITTLE,
+        name="hidden_units_back",
+    )(*operands)
 
 
 def place_kernel(turn, at, *refs):
-    pieces, outs = refs[:4], refs[4:]
+    pieces, out = refs[:4], refs[4]
     p = pl.program_id(0)
     for k in range(4):
 
         @pl.when(p == k)
         def _(k=k):
-            left = 0
-            for out in outs:
-                if turn:
-                    out[...] = pieces[k][...].astype(F32).T
-                else:
-                    wide = out.shape[1]
-                    out[...] = pieces[k][:, left : left + wide].astype(F32)
-                    left += wide
-
-
-def place(pieces, here, splits, turn=False):
+            piece = pieces[k][...].astype(F32)
+            out[...] = piece.T if turn else piece
+
+
+def place(pieces, here, turn=False):
     rows, cols = pieces[0].shape
-    tile = min(rows, 128)
+    tile = min(rows, 256)
     steps = rows // tile
 
     def taken(k):
         return lambda p, i, at: (jnp.where(p == k, i, jnp.where(p > k, steps - 1, 0)), 0)
 
     if turn:
-        out_specs = [pl.BlockSpec((cols, tile), lambda p, i, at: (p ^ at[0], i))]
-        out_shape = [jax.ShapeDtypeStruct((4 * cols, rows), F32)]
+        out_spec = pl.BlockSpec((cols, tile), lambda p, i, at: (p ^ at[0], i))
+        out_shape = jax.ShapeDtypeStruct((4 * cols, rows), F32)
     else:
-        out_specs = [pl.BlockSpec((tile, s), lambda p, i, at: (i, p ^ at[0])) for s in splits]
-        out_shape = [jax.ShapeDtypeStruct((rows, 4 * s), F32) for s in splits]
+        out_spec = pl.BlockSpec((tile, cols), lambda p, i, at: (i, p ^ at[0]))
+        out_shape = jax.ShapeDtypeStruct((rows, 4 * cols), F32)
     return pl.pallas_call(
         functools.partial(place_kernel, turn),
         grid_spec=pltpu.PrefetchScalarGridSpec(
             num_scalar_prefetch=1,
             grid=(4, steps),
             in_specs=[pl.BlockSpec((tile, cols), taken(k)) for k in range(4)],
-            out_specs=out_specs,
+            out_specs=out_spec,
         ),
         out_shape=out_shape,
         compiler_params=pltpu.CompilerParams(vmem_limit_bytes=32 << 20),
+        cost_estimate=pl.CostEstimate(flops=0, bytes_accessed=12 * rows * cols * 4, transcendentals=0),
         name="place",
+    )(here, *pieces)
+
+
+def place_heads_kernel(wide, at, *refs):
+    pieces, (q_ref, k_ref, v_ref, o_ref) = refs[:4], refs[4:]
+    p = pl.program_id(0)
+    to = p ^ at[0]
+    group = lax.broadcasted_iota(jnp.int32, k_ref.shape, 1) // 64
+    for k in range(4):
+
+        @pl.when(p == k)
+        def _(k=k):
+            q_ref[...] = pieces[k][:wide, :].astype(F32).T
+            o_ref[...] = pieces[k][wide + 128 :, :].astype(F32)
+            both = pieces[k][wide : wide + 128, :].astype(F32).T
+            for ref, left in ((k_ref, 0), (v_ref, 64)):
+                spread = jnp.concatenate([both[:, left : left + 64]] * 4, axis=1)
+                ref[...] = spread if k == 0 else jnp.where(group == to, spread, ref[...])
+
+
+def place_heads(pieces, here, wide):
+    cols, rows = pieces[0].shape
+    whole = lambda shape: pl.BlockSpec(shape, lambda p, at: (0, 0))
+    made = lambda *s: jax.ShapeDtypeStruct(s, F32)
+    return pl.pallas_call(
+        functools.partial(place_heads_kernel, wide),
+        grid_spec=pltpu.PrefetchScalarGridSpec(
+            num_scalar_prefetch=1,
+            grid=(4,),
+            in_specs=[whole((cols, rows))] * 4,
+            out_specs=[
+                pl.BlockSpec((rows, wide), lambda p, at: (0, p ^ at[0])),
+                whole((rows, 256)),
+                whole((rows, 256)),
+                pl.BlockSpec((wide, rows), lambda p, at: (p ^ at[0], 0)),
+            ],
+        ),
+        out_shape=[made(rows, 4 * wide), made(rows, 256), made(rows, 256), made(4 * wide, rows)],
+        compiler_params=pltpu.CompilerParams(vmem_limit_bytes=32 << 20),
+        cost_estimate=LITTLE,
+        name="place_heads",
     )(here, *pieces)
 
 
@@ -596,35 +818,38 @@
         axis=0,
     )
     small_all = lax.all_gather(small, "shard", axis=0)
-    downs = small_all[:, : 3 * rank].transpose(1, 0, 2).reshape(3 * rank, width)
-    out_up_all = small_all[:, 24:32].transpose(1, 0, 2).reshape(rank, width)
+    low_in = small_all[:, : 4 * rank].transpose(1, 0, 2).reshape(4 * rank, width)
+    downs, out_up_all = low_in[: 3 * rank], low_in[3 * rank :]
     gain_one = small_all[:, 32].reshape(width).astype(F32)
     gain_two = small_all[:, 33].reshape(width).astype(F32)
     query_up_all = small_all[:, 34].reshape(shards, rank, heads, hs).transpose(1, 2, 0, 3).reshape(rank, wide)
     both_up = small_all[:, 35, : ds // 2].reshape(shards, 2, rank, hs).transpose(1, 2, 0, 3).reshape(2, rank, 64)
-    out_down_all = small_all[:, 36].reshape(shards, heads, hs, rank).transpose(1, 0, 2, 3).reshape(wide, rank)
+    out_down_all = small_all[:, 36].reshape(shards, heads, hs, rank).transpose(3, 1, 0, 2).reshape(rank, wide)
     maps_q = small_all[:, 37:45].reshape(shards, heads, hs, 64).transpose(1, 0, 2, 3).reshape(heads, 64, 64)
     mk = small_all[:, 45:47].reshape(64, 64)
     mq = on_diagonal(maps_q)
-    ups = jnp.zeros((3 * rank, wide + 128), BF)
-    ups = ups.at[:rank, :wide].set(query_up_all)
-    ups = ups.at[rank : 2 * rank, wide : wide + 64].set(both_up[0])
-    ups = ups.at[2 * rank :, wide + 64 :].set(both_up[1])
-
-    w_in_own = jnp.concatenate([mine(query_weight, 1), mine(key_matrix, 1), mine(value_matrix, 1)], axis=1)
-    w_in = gathered(w_in_own)
-    w_out = lax.all_gather(mine(out_weight, 0), "shard", axis=0)
+    low_out = jnp.zeros((4 * rank, 2 * wide + 128), BF)
+    low_out = low_out.at[:rank, :wide].set(query_up_all)
+    low_out = low_out.at[rank : 2 * rank, wide : wide + 64].set(both_up[0])
+    low_out = low_out.at[2 * rank : 3 * rank, wide + 64 : wide + 128].set(both_up[1])
+    low_out = low_out.at[3 * rank :, wide + 128 :].set(out_down_all)
+    ups = low_out[: 3 * rank, : wide + 128]
+
+    w_attn = gathered(
+        jnp.concatenate(
+            [mine(query_weight, 1), mine(key_matrix, 1), mine(value_matrix, 1), mine(out_weight, 0).T], axis=1
+        )
+    )
     w_gu_own = jnp.concatenate([mine(gate_weight, 1), mine(up_weight, 1)], axis=1)
     w_gu = gathered(w_gu_own)
     w_dt = gathered(mine(down_weight, 0).T)
 
-    w_in_eff = (w_in.astype(F32) + dot_tn(downs, ups)).astype(BF)
-    w_out_eff = (
-        w_out.transpose(1, 0, 2).reshape(wide, width).astype(F32) + dot(out_down_all, out_up_all)
-    ).astype(BF)
-
-    h_in = gather_plane(rows_in, rows_in_y)
-    cot = gather_plane(cot_own, cot_y)
+    w_eff = (w_attn.astype(F32) + dot_tn(low_in, low_out)).astype(BF)
+    w_eff = with_layout_constraint(w_eff, Layout(major_to_minor=(0, 1)))
+    w_in_eff, w_out_t = w_eff[:, : wide + 128], w_eff[:, wide + 128 :]
+
+    h_pieces, late = gather_plane(rows_in, rows_in_y)
+    h_in = jnp.concatenate(h_pieces, axis=0)
 
     inv_freq = ROPE_BASE ** (-(np.arange(32, dtype=np.float64) * 2.0) / 64)
     angle = np.arange(slots, dtype=np.float64)[:, None] * inv_freq[None, :]
@@ -641,51 +866,51 @@
     normed = (h_wide * scale_of(h_wide) * gain_one).astype(BF)
     lin = dot(normed, w_in_eff)
     mixed, *saved = attention_forward(lin, cos, sin, mq, mk, perm, seq_lengths)
+    cot_pieces, cot_late = gather_plane(after(cot_own, *late), after(cot_y, *late), (mixed,))
+    cot = jnp.concatenate(cot_pieces, axis=0)
 
     half = slots // 2
-    out_away = dot(mixed[half:], w_out_eff).astype(BF)
-    out_here = dot(mixed[:half], w_out_eff).astype(BF)
-    middle = rows_in.astype(F32) + scatter_plane(out_away, out_here)
+    out_away = dot_nt(mixed[half:], w_out_t).astype(BF)
+    out_here = dot_nt(mixed[:half], w_out_t).astype(BF)
+    out_away, out_here, *_ = lax.optimization_barrier((out_away, out_here, *cot_late))
+    middle = rows_in.astype(F32) + Scatter(out_away, out_here).step().last().own()
     scale_two = scale_of(middle)
     normed_two_own = (middle * scale_two * gain_two).astype(BF)
-    normed_two = gather_plane(normed_two_own)
-
-    gu = dot(normed_two, w_gu)
-    gate, up = gu[:, :units], gu[:, units:]
-    sig = jax.nn.sigmoid(gate)
-    silu = gate * sig
-    active = (silu * up).astype(BF)
-    active_grad = dot(cot, w_dt)
-    gu_grad = jnp.concatenate(
-        [
-            (active_grad * up * (sig * (1.0 + gate * (1.0 - sig)))).astype(BF),
-            (active_grad * silu).astype(BF),
-        ],
-        axis=1,
-    )
-    n2g_away = dot_nt(gu_grad[half:], w_gu).astype(BF)
-    n2g_here = dot_nt(gu_grad[:half], w_gu).astype(BF)
-    normed_two_grad = scatter_plane(n2g_away, n2g_here)
-
+    n2_pieces, _ = gather_plane(normed_two_own)
+    normed_two = jnp.concatenate(n2_pieces, axis=0)
+
+    active, silu, slope = hidden_units(normed_two, w_gu)
+    dw_dt = dot_tn(cot, active).astype(BF)
+    active = after(active, dw_dt)
     ffn_away = dot_nt(active[half:], w_dt).astype(BF)
     ffn_here = dot_nt(active[:half], w_dt).astype(BF)
-    out_own = (middle + scatter_plane(ffn_away, ffn_here)).astype(BF)
-
-    def both_tp(own):
-        other = to_y(own)
-        first = t == 0
-        return jnp.concatenate([jnp.where(first, own, other), jnp.where(first, other, own)], axis=0)
-
-    outputs = both_tp(out_own)[None]
-
-    dw_dt = dot_tn(cot, active).astype(BF)
-    dw_gu = dot_tn(normed_two, gu_grad).astype(BF)
+    ffn = Scatter(ffn_away, lax.optimization_barrier(ffn_here))
+    cot_a = after(cot, *ffn.first)
+    gu_grad, n2g_away = hidden_units_back(cot_a, silu, slope, w_dt, w_gu, True)
+    ffn.here = after(ffn.here, n2g_away)
+    ffn.step()
+    cot_b = after(cot_a, n2g_away, *ffn.second)
+    gu_grad, n2g_here = hidden_units_back(cot_b, silu, slope, w_dt, w_gu, False, gu_grad)
+    ffn.last()
+    normed_two = after(normed_two, ffn.r1a, ffn.r1b, ffn.r2a, ffn.r2b, n2g_here)
+    dw_gate = dot_tn(normed_two, gu_grad[:, :units]).astype(BF)
+    n2g = Scatter(n2g_away, n2g_here, dw_gate)
+    n2g.step().last()
+    dw_up = dot_tn(after(normed_two, *n2g.second), gu_grad[:, units:]).astype(BF)
+    n2g.here = after(n2g.here, dw_up)
+    normed_two_grad = n2g.own()
 
     def scattered(a):
         return lax.psum_scatter(a, "shard", scatter_dimension=0, tiled=True)
 
     dw_dt_own = scattered(dw_dt)
-    dw_gu_own = scattered(dw_gu)
+    dw_gate_own = scattered(dw_gate)
+    dw_up_own = scattered(dw_up)
+    normed_two_grad = after(normed_two_grad, dw_dt_own)
+
+    def both_tp(own, other):
+        first = t == 0
+        return jnp.concatenate([jnp.where(first, own, other), jnp.where(first, other, own)], axis=0)[None]
 
     def norm_back(rows, scale, gain, grad):
         n = rows * scale
@@ -693,23 +918,25 @@
         return scale * (u - n * jnp.mean(u * n, axis=-1, keepdims=True))
 
     middle_grad = cot_own.astype(F32) + norm_back(middle, scale_two, gain_two, normed_two_grad)
-    branch = gather_plane(middle_grad.astype(BF))
-    dmix = dot_nt(branch, w_out_eff)
-    dlin, dmq, dmk = attention_backward(dmix, saved, cos, sin, mq, mk, perm, seq_lengths)
-    n1g_away = dot_nt(dlin[half:], w_in_eff).astype(BF)
-    n1g_here = dot_nt(dlin[:half], w_in_eff).astype(BF)
-    normed_grad = scatter_plane(n1g_away, n1g_here)
-    own_wide = rows_in.astype(F32)
-    in_own = middle_grad + norm_back(own_wide, scale_of(own_wide), gain_one, normed_grad)
-    input_grad = both_tp(in_own.astype(BF)).astype(F32)[None]
-
-    dw_out_t = dot_tn(branch, mixed)
-    dw_in = dot_tn(normed, dlin)
-    dw_out_low, dw_in_low = dw_out_t.astype(BF), dw_in.astype(BF)
-    dw_attn_own = scattered(jnp.concatenate([dw_in_low, dw_out_low], axis=1))
-
-    d_ups = dot(downs, dw_in_low)
-    d_out_down = dot(out_up_all, dw_out_low)
+
+    def rows_out(first_arrival):
+        ffn.here = after(ffn.here, first_arrival)
+        return ((middle + ffn.own()).astype(BF),)
+
+    kept = []
+    branch_pieces, branch_late = gather_plane(
+        middle_grad.astype(BF), later=lambda c0: kept.extend(rows_out(c0)) or kept
+    )
+    (out_own,) = kept
+    dt_pieces = on_ctx(after(dw_dt_own, *branch_late))
+    gate_pieces = on_ctx(after(dw_gate_own, *branch_late))
+    out_other = to_y(out_own)
+    mk_b = after(mk, dw_dt_own, dw_gate_own, out_own)
+    n1g_away, n1g_here, dw_attn, d_low, dmq, dmk = attention_backward(
+        branch_pieces, w_eff, low_in, normed, mixed, shards, saved, cos, sin, mq, mk_b, perm, k, seq_lengths
+    )
+    n1g_away, n1g_here, *_ = lax.optimization_barrier((n1g_away, n1g_here, dt_pieces[2], gate_pieces[2], out_other))
+    d_ups, d_out_down = d_low[: 3 * rank, : wide + 128], d_low[3 * rank :, wide + 128 :]
     by_shard = lambda a: a.astype(BF).reshape(shards, -1, ds)
     d_qu = d_ups[:rank, :wide].reshape(rank, heads, shards, hs).transpose(2, 0, 1, 3)
     d_ku = d_ups[rank : 2 * rank, wide : wide + 64].reshape(rank, shards, hs).transpose(1, 0, 2)
@@ -730,37 +957,57 @@
         ],
         axis=1,
     )
-    d_small_own = lax.psum_scatter(d_small, "shard", scatter_dimension=0, tiled=True)[0]
-
-    dw_in_own = dw_attn_own[:, : wide + 128].astype(F32)
-    dw_out_own = dw_attn_own[:, wide + 128 :]
-    w_in_eff_own = lax.dynamic_slice_in_dim(w_in_eff, s * ds, ds, 0).astype(F32)
+
+    n1g = Scatter(n1g_away, n1g_here, d_small)
+    d_small_own = scatter_shards(d_small, shards).astype(BF)
+    here = c.astype(jnp.int32)[None]
+    down_grad = place([after(p, *n1g.first) for p in dt_pieces], here, turn=True)
+    n1g.here = after(n1g.here, down_grad, d_small_own)
+    n1g.step().last()
+    gate_grad = place([after(p, *n1g.second) for p in gate_pieces], here)
+    small_pieces = on_ctx(after(d_small_own, n1g.r1b))
+    n1g.here = after(n1g.here, gate_grad)
+
+    normed_grad = n1g.own()
+    own_wide = rows_in.astype(F32)
+    in_own = middle_grad + norm_back(own_wide, scale_of(own_wide), gain_one, normed_grad)
+    in_low = after(in_own.astype(BF), dw_up_own)
+    in_first, in_second = to_y(in_low[: piece // 2]), to_y(in_low[piece // 2 :])
+    in_other = jnp.concatenate([in_first, in_second], axis=0)
+    dw_attn_own = lax.psum_scatter(after(dw_attn, dw_up_own), "shard", scatter_dimension=0, tiled=True)[0]
+    dw_attn_own = after(dw_attn_own, in_first)
+    attn_pieces = on_ctx(dw_attn_own)
+    attn_pieces[2] = after(attn_pieces[2], in_second)
+    attn_pieces[3] = to_core(attn_pieces[2])
+    input_grad = both_tp(in_low, after(in_other, attn_pieces[1])).astype(F32)
+    outputs = both_tp(out_own, after(out_other, attn_pieces[1]))
+
+    dw_in_own, dw_out_own = dw_attn_own[: wide + 128], dw_attn_own[wide + 128 :]
+    w_in_eff_own = lax.dynamic_slice_in_dim(w_eff, s * ds, ds, 0)[:, : wide + 128]
     gain_one_own, gain_two_own = attn_gain.astype(F32), ffn_gain.astype(F32)
-    d_gain_one = jnp.sum(w_in_eff_own * dw_in_own, axis=1) / gain_one_own
-    d_gain_two = jnp.sum(w_gu_own.astype(F32) * dw_gu_own.astype(F32), axis=1) / gain_two_own
+    d_gain_one = jnp.sum(w_in_eff_own.T.astype(F32) * dw_in_own.astype(F32), axis=0) / gain_one_own
+    products = lambda w, dw: jnp.sum(w.astype(F32) * after(dw, in_low).astype(F32), axis=1)
+    d_gain_two = (products(w_gu_own[:, :units], dw_gate_own) + products(w_gu_own[:, units:], dw_up_own)) / gain_two_own
     partial = jnp.concatenate(
         [
-            dot_nt(ups, dw_attn_own[:, : wide + 128]),
-            lax.dot_general(out_down_all, dw_out_own, (((0,), (1,)), ((), ())), preferred_element_type=F32),
+            dot(ups, dw_in_own),
+            dot(out_down_all, dw_out_own),
             d_gain_one[None],
             d_gain_two[None],
         ],
         axis=0,
     )
     partial = partial + to_core(partial)
+    partial = after(partial, in_first)
+    partial = partial + to_y(partial)
+    partial_b = partial
     partial = partial + to_x(partial)
-    partial = partial + to_y(partial)
-
-    here = c.astype(jnp.int32)[None]
-    gate_grad, up_grad = place(on_ctx(dw_gu_own), here, (units, units))
-    (down_grad,) = place(on_ctx(dw_dt_own), here, (), turn=True)
-    attn = absolute(on_ctx(dw_attn_own), x, k)
-    side = lambda a, b: jnp.concatenate([p[:, a:b] for p in attn], axis=1).astype(F32)
-    query_weight_grad = side(0, wide)
-    key_weight_grad = side(wide, wide + 64)
-    value_weight_grad = side(wide + 64, wide + 128)
-    out_weight_grad = side(wide + 128, 2 * wide + 128).T
-    smalls = jnp.stack(absolute(on_ctx(d_small_own), x, k)).astype(F32)
+
+    up_grad = place([after(p, in_other) for p in on_ctx(after(dw_up_own, n1g.r1b, n1g.r2a))], here)
+    query_weight_grad, key_weight_grad, value_weight_grad, out_weight_grad = place_heads(
+        [after(p, up_grad, partial_b) for p in attn_pieces], here, wide
+    )
+    smalls = jnp.stack(absolute(small_pieces, x, k)).astype(F32)
     query_map_grad = smalls[:, :8].reshape(4 * heads, hs, 64)
     key_map_grad = smalls[:, 8:10].reshape(4, hs, 64)
     query_up_grad = smalls[:, 10].reshape(4, rank, heads, hs).transpose(1, 0, 2, 3).reshape(rank, 4 * heads, hs)

time: 893 us -> 690 us (0.77)
  waiting for transfers between devices: 370 us -> 180 us
  matrix products: 185 us -> 73.9 us
  Pallas kernels: 76.3 us -> 168 us
  other arithmetic: 57 us -> 83.5 us
  local copies, waits for them, and re-layouts: 102 us -> 84.4 us
    ppermute x25 -> x26, waiting for transfers between devices: 159 us -> 54.5 us  [to_x(): return lax.ppermute(a, 'ctx', ALONG_X)]
    reduce_scatter x3, waiting for transfers between devices: 82.1 us -> 0.01 us  [scattered(): return lax.psum_scatter(a, 'shard', scatter_dimension=0, tiled=True)]
    pallas_call x0 -> x4, Pallas kernels: none -> 67.1 us  [the longest x2 39.6 us: hidden_units_back(): pl.pallas_call(units_back_kernel, grid=(steps,), in_specs=in_specs, out_s...]
    dot_general x8 -> x3, matrix products: 67.2 us -> 11.9 us  [dot(): return jnp.dot(a, b, preferred_element_type=F32)]
    dot_general x8 -> x4, matrix products: 65.9 us -> 16.7 us  [dot_nt(): lax.dot_general(a, b, (((1,), (1,)), ((), ())), preferred_element_type=F32)]
    pallas_call x1, Pallas kernels: 27.9 us -> 54.4 us  [attention_backward(): pl.pallas_call(functools.partial(backward_kernel, heads), grid_spec=grid,...]
    convert_element_type x15, other arithmetic: 18.2 us -> 41.5 us  [the longest x4 11.6 us: __init__(): self.at(*s).astype(BF)]
    unnamed x212 -> x192, local copies, waits for them, and re-layouts: 62.2 us -> 46.1 us
  transfers between devices with their start and end apart: 87 -> 93, of which waited for: 34 -> 31; matrix products, arithmetic and copies ran while one was open for 33% -> 33% of each run, Pallas kernels for 7% -> 24%
where the time goes in v1:
time: 690 us; the launch traced here: 684 us
  waiting for transfers between devices  180 us (26%)
  Pallas kernels  168 us (24%)
  local copies, waits for them, and re-layouts  84.4 us (12%)
  other arithmetic  83.5 us (12%)
  matrix products  73.9 us (11%)
  starting transfers between devices  61.4 us (9%)
  between operations  16.7 us (2%)
  blocking collectives  15.8 us (2%)
    ppermute x22, waiting for transfers between devices, to_y(): return lax.ppermute(a, 'tp', ALONG_Y)  99.4 us
    ppermute x26, waiting for transfers between devices, to_x(): return lax.ppermute(a, 'ctx', ALONG_X)  54.5 us
    pallas_call x1, Pallas kernels, attention_backward(): pl.pallas_call(functools.partial(backward_kernel, heads), grid_spec=grid,...  54.4 us
    unnamed x192, local copies, waits for them, and re-layouts  46.1 us
    dot_general x4, matrix products, dot_tn(): lax.dot_general(a, b, (((0,), (0,)), ((), ())), preferred_element_type=F32)  45.4 us
    pallas_call x2, Pallas kernels, hidden_units_back(): pl.pallas_call(units_back_kernel, grid=(steps,), in_specs=in_specs, out_s...  39.6 us
    ppermute x26, starting transfers between devices, to_x(): return lax.ppermute(a, 'ctx', ALONG_X)  27.7 us
    pallas_call x1, Pallas kernels, attention_forward(): pl.pallas_call(functools.partial(forward_kernel, heads), grid_spec=grid,...  24.8 us
  transfers between devices with their start and end apart: 93, of which 31 were waited for; matrix products, arithmetic and copies ran while one was open for 33% of the time, Pallas kernels for 24%

profile of v1, /device:TPU:0, one launch (start us, length us, event | category | flops | bytes accessed | tf_op | source)
XLA Modules:
  0.0 684.5 jit_solution(13173659820079900447)
XLA Ops:
  26.5 15.8 %all-gather = bf16[192,512]{1,0:T(8,128)(2,1)S(1)} all-gather(bf16[48,512]{1,0:T(8,128)(2,1)S(1)} %concatenate.89), channel_id=2, replica_groups=mesh['shard'=4,'ctx'=4,'tp'=2] {'shard'}, dimensions={0}, use_global_device_ids=true | all-gather | bytes 245760 | tf_op jit(solution)/shard_map/all_gather | solution.py:820
  88.9 8.7 %fusion.2.refs_12_ = bf16[2048,2048]{1,0:T(8,128)(2,1)} fusion(bf16[2048,2048]{1,0:T(8,128)(2,1)} %constant_dynamic-update-slice_fusion, f32[2048]{0:T(1024)S(1)} %bitcast.140, f32[2048]{0:T(1024)S(1)} %add_rsqrt_fusion), kind=kLoop, calls=%fused_computation.6 | loop fusion | flops 16777216 | bytes 16793600 | tf_op jit(solution)/shard_map/convert_element_type | solution.py:866
  100.3 9.5 %fusion.24.lin_ref = f32[2048,384]{1,0:T(8,128)} fusion(bf16[2048,2048]{1,0:T(8,128)(2,1)} %fusion.2.refs_12_, bf16[2048,640]{1,0:T(8,128)(2,1)S(1)} %add_convert_fusion.refs_10_), kind=kOutput, calls=%fused_computation.46 | convolution fusion | flops 3221225472 | bytes 13107200 | tf_op jit(solution)/shard_map/dot_general | solution.py:26
  109.8 24.8 %attention_forward.1 = (bf16[2048,256]{1,0:T(8,128)(2,1)S(1)}, f32[2048,256]{1,0:T(8,128)}, f32[2048,256]{1,0:T(8,128)}, bf16[2048,256]{1,0:T(8,128)(2,1)S(1)}, ...) custom-call(s32[8]{0:T(128)S(1)} %xor_add_fusion.perm, ...), custom_call_target="tpu_custom_call" | custom-call | flops 1048576 | bytes 65536 | tf_op jit(solution)/shard_map/attention_forward/pallas_call | solution.py:457
  140.5 9.8 %collective-permute-done.9 = bf16[128,2048]{1,0:T(8,128)(2,1)S(1)} collective-permute-done((bf16[128,2048]{1,0:T(8,128)(2,1)S(1)}, bf16[128,2048]{1,0:T(8,128)(2,1)S(1)}, u32[]{:S(2)}, u32[]{:S(2)}) %collective-permute-start.9) | collective-permute-done | bytes 524320 | tf_op jit(solution)/shard_map/ppermute | solution.py:46
  188.0 8.3 %collective-permute-done.15 = bf16[128,2048]{1,0:T(8,128)(2,1)S(1)} collective-permute-done((bf16[128,2048]{1,0:T(8,128)(2,1)S(1)}, bf16[128,2048]{1,0:T(8,128)(2,1)S(1)}, u32[]{:S(2)}, u32[]{:S(2)}) %collective-permute-start.15) | collective-permute-done | bytes 524320 | tf_op jit(solution)/shard_map/ppermute | solution.py:46
  206.8 18.8 %collective-permute-done.19 = bf16[256,2048]{1,0:T(8,128)(2,1)S(1)} collective-permute-done((bf16[256,2048]{1,0:T(8,128)(2,1)S(1)}, bf16[256,2048]{1,0:T(8,128)(2,1)S(1)}, u32[]{:S(2)}, u32[]{:S(2)}) %collective-permute-start.19) | collective-permute-done | bytes 1048608 | tf_op jit(solution)/shard_map/ppermute | solution.py:46
  245.6 24.2 %hidden_units.1 = (bf16[2048,1024]{1,0:T(8,128)(2,1)}, bf16[2048,1024]{1,0:T(8,128)(2,1)S(1)}, bf16[2048,1024]{1,0:T(8,128)(2,1)S(1)}) custom-call(bf16[2048,2048]{1,0:T(8,128)(2,1)} %constant_dynamic-update-slice_fusion.10.h_ref, bf16[2048,2048]{1,0:T(8,128)(2,1)} %all-gather.7.cloned.1.call-done.w_ref.w_gu_ref), custom_call_target="tpu_custom_call" | custom-call | flops 1048576 | bytes 65536 | tf_op jit(solution)/shard_map/hidden_units/pallas_call | solution.py:582
  273.8 14.0 %convolution_convert_fusion.4 = bf16[2048,1024]{1,0:T(8,128)(2,1)} fusion(bf16[2048,2048]{1,0:T(8,128)(2,1)} %copy-done.31, bf16[2048,1024]{1,0:T(8,128)(2,1)} %get-tuple-element.187), kind=kOutput, calls=%fused_computation.18 | convolution fusion | flops 8592031744 | bytes 16777216 | tf_op jit(solution)/shard_map/dot_general | solution.py:34
  287.9 15.8 %all-gather.9.cloned.1.call-done.w_dt_ref = bf16[2048,1024]{1,0:T(8,128)(2,1)} async-done(((bf16[512,1024]{1,0:T(8,128)(2,1)}), bf16[2048,1024]{1,0:T(8,128)(2,1)}) %all-gather.9.cloned.1.call-update) | async-done | bytes 4194320 | tf_op jit(solution)/shard_map/all_gather | solution.py:790
  303.7 7.5 %convolution_convert_fusion.2 = bf16[1024,2048]{1,0:T(8,128)(2,1)S(1)} fusion(bf16[2048,1024]{1,0:T(8,128)(2,1)} %all-gather.9.cloned.1.call-done.w_dt_ref, bf16[2048,1024]{1,0:T(8,128)(2,1)} %get-tuple-element.187), kind=kOutput, calls=%fused_computation.16 | convolution fusion | flops 4297064448 | bytes 10485760 | tf_op jit(solution)/shard_map/dot_general | solution.py:30
  325.1 20.3 %hidden_units_back.2 = (bf16[2048,2048]{1,0:T(8,128)(2,1)}, bf16[1024,2048]{1,0:T(8,128)(2,1)}) custom-call(bf16[2048,2048]{1,0:T(8,128)(2,1)} %copy-done.31, bf16[2048,1024]{1,0:T(8,128)(2,1)S(1)} %copy-done.3, bf16[2048,1024]{1,0:T(8,128)(2,1)} %copy-done.4, bf16[2048,1024]{1,0:T(8,128)(2,1)} %all-gather.9.cloned.1.call-done.w_dt_ref, ...), custom_call_target="tpu_custom_call" | custom-call | flops 1048576 | bytes 65536 | tf_op jit(solution)/shard_map/hidden_units_back/pallas_call | solution.py:625
  350.3 19.3 %hidden_units_back.3 = (bf16[2048,2048]{1,0:T(8,128)(2,1)}, bf16[1024,2048]{1,0:T(8,128)(2,1)S(1)}) custom-call(bf16[2048,2048]{1,0:T(8,128)(2,1)} %copy-done.31, bf16[2048,1024]{1,0:T(8,128)(2,1)S(1)} %copy-done.3, bf16[2048,1024]{1,0:T(8,128)(2,1)} %copy-done.4, ...), custom_call_target="tpu_custom_call", output_to_operand_aliasing={{0}: (5, {})} | custom-call | flops 1048576 | bytes 65536 | tf_op jit(solution)/shard_map/hidden_units_back/pallas_call | solution.py:625
  371.6 14.5 %fusion.7 = bf16[2048,1024]{1,0:T(8,128)(2,1)} fusion(bf16[2048,2048]{1,0:T(8,128)(2,1)} %constant_dynamic-update-slice_fusion.10.h_ref, bf16[2048,2048]{1,0:T(8,128)(2,1)} %get-tuple-element.203), kind=kOutput, calls=%fused_computation.12 | convolution fusion | flops 8592031744 | bytes 16777216 | tf_op jit(solution)/shard_map/dot_general | solution.py:34
  394.2 10.7 %collective-permute-done.40 = bf16[128,2048]{1,0:T(8,128)(2,1)S(1)} collective-permute-done((bf16[128,2048]{1,0:T(8,128)(2,1)S(1)}, bf16[128,2048]{1,0:T(8,128)(2,1)S(1)}, u32[]{:S(2)}, u32[]{:S(2)}) %collective-permute-start.40) | collective-permute-done | bytes 524320 | tf_op jit(solution)/shard_map/ppermute | solution.py:46
  410.6 14.2 %fusion.10 = bf16[2048,1024]{1,0:T(8,128)(2,1)} fusion(bf16[2048,2048]{1,0:T(8,128)(2,1)} %constant_dynamic-update-slice_fusion.10.h_ref, bf16[2048,2048]{1,0:T(8,128)(2,1)} %get-tuple-element.203), kind=kOutput, calls=%fused_computation.13 | convolution fusion | flops 8592031744 | bytes 16777216 | tf_op jit(solution)/shard_map/dot_general | solution.py:34
  444.6 18.4 %collective-permute-done.49.refs_2_ = bf16[256,2048]{1,0:T(8,128)(2,1)} collective-permute-done((bf16[256,2048]{1,0:T(8,128)(2,1)S(1)}, bf16[256,2048]{1,0:T(8,128)(2,1)}, u32[]{:S(2)}, u32[]{:S(2)}) %collective-permute-start.49) | collective-permute-done | bytes 1048608 | tf_op jit(solution)/shard_map/ppermute | solution.py:46
  468.4 11.1 %collective-permute-done.51.refs_4_ = bf16[128,2048]{1,0:T(8,128)(2,1)} collective-permute-done((bf16[128,2048]{1,0:T(8,128)(2,1)}, bf16[128,2048]{1,0:T(8,128)(2,1)}, u32[]{:S(2)}, u32[]{:S(2)}) %collective-permute-start.51) | collective-permute-done | bytes 524320 | tf_op jit(solution)/shard_map/ppermute | solution.py:42
  487.6 54.4 %attention_backward.1 = (bf16[1024,2048]{1,0:T(8,128)(2,1)}, bf16[1024,2048]{1,0:T(8,128)(2,1)}, bf16[4,640,512]{2,1,0:T(8,128)(2,1)}, f32[32,640]{1,0:T(8,128)S...) custom-call(s32[24]{0:T(128)S(1)} %pad_add_fusion.table, s32[1]{0:T(128)} %copy.156.length, ...), custom_call_target="tpu_custom_call" | custom-call | flops 20000000000 | bytes 16777216 | tf_op jit(solution)/shard_map/attention_backward/pallas_call | solution.py:549
  561.6 7.7 %place.3 = f32[4096,512]{1,0:T(8,128)} custom-call(s32[1]{0:T(128)} %bitcast.33.at, bf16[512,1024]{1,0:T(8,128)(2,1)S(1)} %copy-done.10, bf16[512,1024]{1,0:T(8,128)(2,1)S(1)} %collective-permute-done.59.refs_1_, bf16[512,1024]{1,0:T(8,128)(2,1)} %collective-permute-done.56.refs_2_, bf16[512,1024]{1,0:T(8,128)(2,1)} %collective-permute-done.60.refs_3_), custom_call_target="tpu_custom_call" | custom-call | bytes 25165824 | tf_op jit(solution)/shard_map/place/pallas_call | solution.py:669
  581.4 7.9 %place.4 = f32[512,4096]{1,0:T(8,128)} custom-call(s32[1]{0:T(128)} %bitcast.33.at, bf16[512,1024]{1,0:T(8,128)(2,1)S(1)} %copy-done.7, bf16[512,1024]{1,0:T(8,128)(2,1)} %collective-permute-done.66.refs_1_, bf16[512,1024]{1,0:T(8,128)(2,1)} %collective-permute-done.57.refs_2_, bf16[512,1024]{1,0:T(8,128)(2,1)} %collective-permute-done.67.refs_3_), custom_call_target="tpu_custom_call" | custom-call | bytes 25165824 | tf_op jit(solution)/shard_map/place/pallas_call | solution.py:669
  593.3 9.2 %collective-permute-done.68 = bf16[128,2048]{1,0:T(8,128)(2,1)} collective-permute-done((bf16[128,2048]{1,0:T(8,128)(2,1)}, bf16[128,2048]{1,0:T(8,128)(2,1)}, u32[]{:S(2)}, u32[]{:S(2)}) %collective-permute-start.68) | collective-permute-done | bytes 524320 | tf_op jit(solution)/shard_map/ppermute | solution.py:42
  622.6 14.5 %collective-permute-done.72 = bf16[128,2048]{1,0:T(8,128)(2,1)} collective-permute-done((bf16[128,2048]{1,0:T(8,128)(2,1)}, bf16[128,2048]{1,0:T(8,128)(2,1)}, u32[]{:S(2)}, u32[]{:S(2)}) %collective-permute-start.72) | collective-permute-done | bytes 524320 | tf_op jit(solution)/shard_map/ppermute | solution.py:46
  659.2 7.8 %collective-permute-done.77 = f32[34,512]{1,0:T(8,128)S(1)} collective-permute-done((f32[34,512]{1,0:T(8,128)S(1)}, f32[34,512]{1,0:T(8,128)S(1)}, u32[]{:S(2)}, u32[]{:S(2)}) %collective-permute-start.77) | collective-permute-done | bytes 69664 | tf_op jit(solution)/shard_map/ppermute | solution.py:42
  (541 shorter events, 300.6 us)
Async XLA Ops:
  7.2 90.4 %all-gather.5.cloned.1.call-start = ((), (), s32[]{:S(2)}) async-start(), calls=%async_computation.4 | async-start | bytes 3276800 | tf_op jit(solution)/shard_map/all_gather | solution.py:790
  11.7 233.8 %all-gather.7.cloned.1.call-start = ((), (), s32[]{:S(2)}) async-start(), calls=%async_computation.5 | async-start | bytes 10485760 | tf_op jit(solution)/shard_map/all_gather | solution.py:790
  13.0 63.5 %collective-permute-start.3 = (bf16[256,2048]{1,0:T(8,128)(2,1)S(1)}, bf16[256,2048]{1,0:T(8,128)(2,1)}, u32[]{:S(2)}, u32[]{:S(2)}) collective-permute-start(bf16[256,2048]{1,0:T(8,128)(2,1)S(1)} %get-tuple-element.330), channel_id=1, source_target_pairs={{0,2},{2,0},{4,6},{6,4},{1,3},{3,1},{5,7},{7,5},{8,10},{10,8},{12,... | collective-permute-start | bytes 3145736 | tf_op jit(solution)/shard_map/ppermute | solution.py:38
  13.5 43.8 %collective-permute-start = (bf16[256,2048]{1,0:T(8,128)(2,1)S(1)}, bf16[256,2048]{1,0:T(8,128)(2,1)}, u32[]{:S(2)}, u32[]{:S(2)}) collective-permute-start(bf16[256,2048]{1,0:T(8,128)(2,1)S(1)} %get-tuple-element.330), channel_id=1, source_target_pairs={{0,4},{2,6},{4,0},{6,2},{1,5},{3,7},{5,1},{7,3},{8,12},{10,14},{12... | collective-permute-start | bytes 3145736 | tf_op jit(solution)/shard_map/ppermute | solution.py:42
  16.8 46.8 %collective-permute-start.2 = (bf16[128,2048]{1,0:T(8,128)(2,1)}, bf16[128,2048]{1,0:T(8,128)(2,1)}, u32[]{:S(2)}, u32[]{:S(2)}) collective-permute-start(bf16[128,2048]{1,0:T(8,128)(2,1)} %dynamic-slice_bitcast_fusion.2), channel_id=1, source_target_pairs={{0,4},{2,6},{4,0},{6,2},{1,5},{3,7},{5,1},{7,3},{8,12},{10,14},{12... | collective-permute-start | bytes 1572872 | tf_op jit(solution)/shard_map/ppermute | solution.py:42
  21.5 282.1 %all-gather.9.cloned.1.call-start = ((), (), s32[]{:S(2)}) async-start(), calls=%async_computation.6 | async-start | bytes 5242880 | tf_op jit(solution)/shard_map/all_gather | solution.py:790
  72.3 68.2 %collective-permute-start.10 = (bf16[128,2048]{1,0:T(8,128)(2,1)}, bf16[128,2048]{1,0:T(8,128)(2,1)}, u32[]{:S(2)}, u32[]{:S(2)}) collective-permute-start(bf16[128,2048]{1,0:T(8,128)(2,1)} %slice.474), channel_id=1, source_target_pairs={{0,4},{2,6},{4,0},{6,2},{1,5},{3,7},{5,1},{7,3},{8,12},{10,14},{12... | collective-permute-start | bytes 1572872 | tf_op jit(solution)/shard_map/ppermute | solution.py:42
  78.9 55.8 %collective-permute-start.8 = (bf16[256,2048]{1,0:T(8,128)(2,1)}, bf16[256,2048]{1,0:T(8,128)(2,1)}, u32[]{:S(2)}, u32[]{:S(2)}) collective-permute-start(bf16[256,2048]{1,0:T(8,128)(2,1)} %get-tuple-element.174), channel_id=1, source_target_pairs={{0,4},{2,6},{4,0},{6,2},{1,5},{3,7},{5,1},{7,3},{8,12},{10,14},{12... | collective-permute-start | bytes 3145736 | tf_op jit(solution)/shard_map/ppermute | solution.py:42
  165.4 266.2 %reduce-scatter.5.cloned.1.call-start = ((), (), s32[]{:S(2)}) async-start(), calls=%async_computation.7 | async-start | bytes 5242880 | tf_op jit(solution)/shard_map/reduce_scatter | solution.py:904
  165.5 39.1 %collective-permute-start.27 = (bf16[256,2048]{1,0:T(8,128)(2,1)}, bf16[256,2048]{1,0:T(8,128)(2,1)S(1)}, u32[]{:S(2)}, u32[]{:S(2)}) collective-permute-start(bf16[256,2048]{1,0:T(8,128)(2,1)} %get-tuple-element.174), channel_id=1, source_target_pairs={{0,2},{2,0},{4,6},{6,4},{1,3},{3,1},{5,7},{7,5},{8,10},{10,8},{12,... | collective-permute-start | bytes 3145736 | tf_op jit(solution)/shard_map/ppermute | solution.py:38
  206.6 34.1 %collective-permute-start.22 = (bf16[256,2048]{1,0:T(8,128)(2,1)S(1)}, bf16[256,2048]{1,0:T(8,128)(2,1)S(1)}, u32[]{:S(2)}, u32[]{:S(2)}) collective-permute-start(bf16[256,2048]{1,0:T(8,128)(2,1)S(1)} %get-tuple-element.326), channel_id=1, source_target_pairs={{0,2},{2,0},{4,6},{6,4},{1,3},{3,1},{5,7},{7,5},{8,10},{10,8},{12,... | collective-permute-start | bytes 3145736 | tf_op jit(solution)/shard_map/ppermute | solution.py:38
  287.8 194.8 %reduce-scatter.7.cloned.1.call-start = ((), (), s32[]{:S(2)}) async-start(), calls=%async_computation.8 | async-start | bytes 5242880 | tf_op jit(solution)/shard_map/reduce_scatter | solution.py:904
  324.0 47.6 %collective-permute-start.35 = (bf16[128,2048]{1,0:T(8,128)(2,1)S(1)}, bf16[128,2048]{1,0:T(8,128)(2,1)}, u32[]{:S(2)}, u32[]{:S(2)}) collective-permute-start(bf16[128,2048]{1,0:T(8,128)(2,1)S(1)} %get-tuple-element.190), channel_id=1, source_target_pairs={{0,4},{2,6},{4,0},{6,2},{1,5},{3,7},{5,1},{7,3},{8,12},{10,14},{12... | collective-permute-start | bytes 1572872 | tf_op jit(solution)/shard_map/ppermute | solution.py:42
  324.6 47.0 %collective-permute-start.38 = (bf16[128,2048]{1,0:T(8,128)(2,1)S(1)}, bf16[128,2048]{1,0:T(8,128)(2,1)}, u32[]{:S(2)}, u32[]{:S(2)}) collective-permute-start(bf16[128,2048]{1,0:T(8,128)(2,1)S(1)} %get-tuple-element.191), channel_id=1, source_target_pairs={{0,1},{1,0},{2,3},{3,2},{4,5},{5,4},{6,7},{7,6},{8,9},{9,8},{10,11... | collective-permute-start | bytes 1572872 | tf_op jit(solution)/shard_map/ppermute | solution.py:46
  350.3 35.9 %collective-permute-start.39 = (bf16[1024,2048]{1,0:T(8,128)(2,1)}, bf16[1024,2048]{1,0:T(8,128)(2,1)}, u32[]{:S(2)}, u32[]{:S(2)}) collective-permute-start(bf16[1024,2048]{1,0:T(8,128)(2,1)} %get-tuple-element.195), channel_id=1, source_target_pairs={{0,2},{2,0},{4,6},{6,4},{1,3},{3,1},{5,7},{7,5},{8,10},{10,8},{12,... | collective-permute-start | bytes 12582920 | tf_op jit(solution)/shard_map/ppermute | solution.py:38
  386.2 164.3 %reduce-scatter.9.cloned.1.call-start = ((), (), s32[]{:S(2)}) async-start(), calls=%async_computation.9 | async-start | bytes 5242880 | tf_op jit(solution)/shard_map/reduce_scatter | solution.py:904
  391.2 33.6 %collective-permute-start.42 = (bf16[128,2048]{1,0:T(8,128)(2,1)}, bf16[128,2048]{1,0:T(8,128)(2,1)}, u32[]{:S(2)}, u32[]{:S(2)}) collective-permute-start(bf16[128,2048]{1,0:T(8,128)(2,1)} %get-tuple-element.211), channel_id=1, source_target_pairs={{0,4},{2,6},{4,0},{6,2},{1,5},{3,7},{5,1},{7,3},{8,12},{10,14},{12... | collective-permute-start | bytes 1572872 | tf_op jit(solution)/shard_map/ppermute | solution.py:42
  392.7 32.1 %collective-permute-start.45 = (bf16[128,2048]{1,0:T(8,128)(2,1)}, bf16[128,2048]{1,0:T(8,128)(2,1)}, u32[]{:S(2)}, u32[]{:S(2)}) collective-permute-start(bf16[128,2048]{1,0:T(8,128)(2,1)} %get-tuple-element.212), channel_id=1, source_target_pairs={{0,1},{1,0},{2,3},{3,2},{4,5},{5,4},{6,7},{7,6},{8,9},{9,8},{10,11... | collective-permute-start | bytes 1572872 | tf_op jit(solution)/shard_map/ppermute | solution.py:46
  437.1 199.9 %reduce-scatter.11.cloned.1.call-start = ((), (), s32[]{:S(2)}) async-start(), calls=%async_computation.10 | async-start | bytes 3276800 | tf_op jit(solution)/shard_map/reduce_scatter | solution.py:977
  481.9 60.8 %collective-permute-start.47 = (bf16[256,2048]{1,0:T(8,128)(2,1)}, bf16[256,2048]{1,0:T(8,128)(2,1)}, u32[]{:S(2)}, u32[]{:S(2)}) collective-permute-start(bf16[256,2048]{1,0:T(8,128)(2,1)} %fusion.21), channel_id=1, source_target_pairs={{0,1},{1,0},{2,3},{3,2},{4,5},{5,4},{6,7},{7,6},{8,9},{9,8},{10,11... | collective-permute-start | bytes 3145736 | tf_op jit(solution)/shard_map/ppermute | solution.py:46
  482.7 60.1 %collective-permute-start.56 = (bf16[512,1024]{1,0:T(8,128)(2,1)S(1)}, bf16[512,1024]{1,0:T(8,128)(2,1)}, u32[]{:S(2)}, u32[]{:S(2)}) collective-permute-start(bf16[512,1024]{1,0:T(8,128)(2,1)S(1)} %copy-done.10), channel_id=1, source_target_pairs={{0,4},{2,6},{4,0},{6,2},{1,5},{3,7},{5,1},{7,3},{8,12},{10,14},{12... | collective-permute-start | bytes 3145736 | tf_op jit(solution)/shard_map/ppermute | solution.py:42
  484.3 58.4 %collective-permute-start.57 = (bf16[512,1024]{1,0:T(8,128)(2,1)}, bf16[512,1024]{1,0:T(8,128)(2,1)}, u32[]{:S(2)}, u32[]{:S(2)}) collective-permute-start(bf16[512,1024]{1,0:T(8,128)(2,1)} %reduce-scatter.7.cloned.1.call-done.refs_0_), channel_id=1, source_target_pairs={{0,4},{2,6},{4,0},{6,2},{1,5},{3,7},{5,1},{7,3},{8,12},{10,14},{12... | collective-permute-start | bytes 3145736 | tf_op jit(solution)/shard_map/ppermute | solution.py:42
  602.5 50.1 %collective-permute-start.78 = (bf16[512,1024]{1,0:T(8,128)(2,1)S(1)}, bf16[512,1024]{1,0:T(8,128)(2,1)}, u32[]{:S(2)}, u32[]{:S(2)}) collective-permute-start(bf16[512,1024]{1,0:T(8,128)(2,1)S(1)} %copy-done.6), channel_id=1, source_target_pairs={{0,2},{2,0},{4,6},{6,4},{1,3},{3,1},{5,7},{7,5},{8,10},{10,8},{12,... | collective-permute-start | bytes 3145736 | tf_op jit(solution)/shard_map/ppermute | solution.py:38
  611.1 39.7 %collective-permute-start.74 = (bf16[128,2048]{1,0:T(8,128)(2,1)}, bf16[128,2048]{1,0:T(8,128)(2,1)}, u32[]{:S(2)}, u32[]{:S(2)}) collective-permute-start(bf16[128,2048]{1,0:T(8,128)(2,1)} %get-tuple-element.369), channel_id=1, source_target_pairs={{0,1},{1,0},{2,3},{3,2},{4,5},{5,4},{6,7},{7,6},{8,9},{9,8},{10,11... | collective-permute-start | bytes 1572872 | tf_op jit(solution)/shard_map/ppermute | solution.py:46
  (148 other events, 2493.8 us)
Sparse Core Ops, SparseCore 0:
  11.8 60.5 all-gather.4
  74.6 148.3 all-gather.6
  224.6 79.0 all-gather.8
  305.8 75.2 reduce-scatter.4
  386.3 74.3 reduce-scatter.6
  462.8 77.2 reduce-scatter.8
  550.6 50.2 reduce-scatter.10

commit v2 on v1

--- a/solution.py
+++ b/solution.py
@@ -63,6 +63,18 @@
     cx, cy = to_core(px), to_core(py)
     caxy, cbxy = to_core(axy), to_core(bxy)
     return [own, px, py, axy, bxy, c0, cx, cy, caxy, cbxy], (axy, bxy)
+
+
+def gather_halves(own, later):
+    a, b = own
+    pxa, pxb = to_x(a), to_x(b)
+    c0 = [to_core(a), to_core(b)]
+    pyb, pya = to_y(b), to_y(a)
+    later = later(c0[0])
+    bxy, axy = to_x(after(pyb, *later)), to_y(after(pxa, *later))
+    pxb, pya = after(pxb, *later), after(pya, *later)
+    rest = [pxa, pxb, pya, pyb, axy, bxy]
+    return [a, b, *rest, *c0, *(to_core(r) for r in rest)], (axy, bxy)
 
 
 class Scatter:
@@ -260,7 +272,7 @@
     length,
     *refs,
 ):
-    pieces, refs = refs[:10], refs[10:]
+    pieces, refs = refs[:16], refs[16:]
     (w_ref,
     low_ref,
     normed_ref,
@@ -305,15 +317,12 @@
     blocks = rows // BLOCK
     wide = heads * 64
     r_here = table[i]
-    for n, held in enumerate(((0,), (1,), (2,), (3, 4), (5,), (6,), (7,), (8, 9))):
+    for n in range(8):
 
         @pl.when(r_here == n)
-        def _(held=held):
-            if len(held) == 1:
-                branch_ref[...] = pieces[held[0]][...]
-            else:
-                branch_ref[:half, :] = pieces[held[0]][...]
-                branch_ref[half:, :] = pieces[held[1]][...]
+        def _(n=n):
+            branch_ref[:half, :] = pieces[2 * n][...]
+            branch_ref[half:, :] = pieces[2 * n + 1][...]
 
     dmix_ref[...] = dot(branch_ref[...], w_ref[:, wide + 128 :])
 
@@ -413,10 +422,10 @@
         dlow_ref[...] = dot_nt(low_ref[...], low)
 
 
-def attention_forward(lin, cos, sin, mq, mk, perm, seq_lengths):
+def attention_forward(lin, cos, sin, mq, mk, table, seq_lengths):
     slots, cols = lin.shape
     heads = (cols - 128) // 64
-    pieces = perm.shape[0]
+    pieces = table.shape[0] // 3
     rows = slots // pieces
     blocks = rows // BLOCK
     wide = heads * 64
@@ -472,22 +481,19 @@
         compiler_params=pltpu.CompilerParams(vmem_limit_bytes=48 << 20),
         cost_estimate=LITTLE,
         name="attention_forward",
-    )(perm, seq_lengths, lin, cos, sin, mq, mk)
-
-
-def attention_backward(branch_pieces, w_eff, low_in, normed, mixed, shards, saved, cos, sin, mq, mk, perm, k, seq_lengths):
+    )(table, seq_lengths, lin, cos, sin, mq, mk)
+
+
+def attention_backward(branch_pieces, w_eff, low_in, normed, mixed, shards, saved, cos, sin, mq, mk, table, seq_lengths):
     mix, rden, q, kv, qf, kf, a, st, norm = saved
     slots, wide = mix.shape
     width = w_eff.shape[0]
     heads = wide // 64
-    pieces = perm.shape[0]
+    pieces = table.shape[0] // 3
     rows = slots // pieces
     blocks = rows // BLOCK
     span = heads * rows
     last = pieces - 1
-    back = perm[::-1] & 3
-    one, two = back[np.array([0, 1, 1, 1, 4, 5, 5, 5])], back[np.array([2, 2, 2, 3, 3, 3, 6, 7])]
-    table = jnp.concatenate([perm, jnp.where(k == 0, one, two), jnp.where(k == 0, two, one)])
     moved = lambda g, table, length: (table[last - g], 0)
     plain = lambda g, table, length: (last - g, 0)
     prior = lambda g, table, length: (jnp.maximum((last - g) * blocks - 1, 0), 0)
@@ -558,9 +564,73 @@
             made(64, 64, F32),
         ],
         compiler_params=pltpu.CompilerParams(vmem_limit_bytes=48 << 20),
-        cost_estimate=pl.CostEstimate(flops=2 * 10**10, bytes_accessed=16 << 20, transcendentals=0),
+        cost_estimate=pl.CostEstimate(flops=5 * 10**10, bytes_accessed=16 << 20, transcendentals=0),
         name="attention_backward",
     )(table, seq_lengths, *branch_pieces, w_eff, low_in, normed, mixed, mix, rden, q, kv, kv, qf, kf, kf, a, st, norm, cos, sin, mq, mk)
+
+
+def norm_back_kernel(side, here, got, r1a, r2a, r1b, r2b, rows_ref, gain_ref, base_ref, low_a, low_b, *wide):
+    i = pl.program_id(0)
+
+    def through(r1, r2, out):
+        grad = here[...].astype(F32) + got[...].astype(F32) + r1[...].astype(F32) + r2[...].astype(F32)
+        rows = rows_ref[...].astype(F32)
+        scale = lax.rsqrt(jnp.mean(rows * rows, axis=1, keepdims=True) + EPSILON)
+        n = rows * scale
+        u = grad * gain_ref[...]
+        total = base_ref[...].astype(F32) + scale * (u - n * jnp.mean(u * n, axis=1, keepdims=True))
+        out[...] = total.astype(BF)
+        for w in wide:
+            w[...] = total
+
+    @pl.when(i < side)
+    def _():
+        through(r1a, r2a, low_a)
+
+    @pl.when(i >= side)
+    def _():
+        through(r1b, r2b, low_b)
+
+
+def norm_back(scattered, rows, gain, base, keep):
+    count, width = rows.shape
+    side = 2
+    tile = count // 2 // side
+    at = lambda i: (i, 0)
+    first = lambda i: (jnp.minimum(i, side - 1), 0)
+    second = lambda i: (jnp.maximum(i - side, 0), 0)
+    block = lambda index: pl.BlockSpec((tile, width), index)
+    half = jax.ShapeDtypeStruct((count // 2, width), BF)
+    return pl.pallas_call(
+        functools.partial(norm_back_kernel, side),
+        grid=(2 * side,),
+        in_specs=[
+            block(at),
+            block(at),
+            block(first),
+            block(first),
+            block(second),
+            block(second),
+            block(at),
+            pl.BlockSpec((1, width), lambda i: (0, 0)),
+            block(at),
+        ],
+        out_specs=[block(first), block(second)] + [block(at)] * keep,
+        out_shape=[half, half] + [jax.ShapeDtypeStruct((count, width), F32)] * keep,
+        compiler_params=pltpu.CompilerParams(vmem_limit_bytes=24 << 20),
+        cost_estimate=pl.CostEstimate(flops=0, bytes_accessed=12 << 20, transcendentals=0),
+        name="norm_back",
+    )(
+        scattered.here,
+        scattered.got,
+        scattered.r1a,
+        scattered.r2a,
+        scattered.r1b,
+        scattered.r2b,
+        rows,
+        gain[None],
+        base,
+    )
 
 
 def units_kernel(h_ref, w_ref, active_ref, silu_ref, slope_ref):
@@ -636,7 +706,7 @@
         ],
         input_output_aliases={} if grads is None else {5: 0},
         compiler_params=pltpu.CompilerParams(vmem_limit_bytes=44 << 20),
-        cost_estimate=LITTLE,
+        cost_estimate=pl.CostEstimate(flops=3 * rows * width * units, bytes_accessed=24 << 20, transcendentals=0),
         name="hidden_units_back",
     )(*operands)
 
@@ -858,6 +928,9 @@
     order = np.arange(8)
     perm = (((order >> 1) & 1) ^ k) * 4 + ((order & 1) ^ t) * 2 + ((order >> 2) ^ x)
     perm = perm.astype(jnp.int32)
+    back = perm[::-1] & 3
+    one, two = back[np.array([0, 1, 1, 1, 4, 5, 5, 5])], back[np.array([2, 2, 2, 3, 3, 3, 6, 7])]
+    table = jnp.concatenate([perm, jnp.where(k == 0, one, two), jnp.where(k == 0, two, one)])
 
     def scale_of(rows):
         return lax.rsqrt(jnp.mean(rows * rows, axis=-1, keepdims=True) + EPSILON)
@@ -865,7 +938,7 @@
     h_wide = h_in.astype(F32)
     normed = (h_wide * scale_of(h_wide) * gain_one).astype(BF)
     lin = dot(normed, w_in_eff)
-    mixed, *saved = attention_forward(lin, cos, sin, mq, mk, perm, seq_lengths)
+    mixed, *saved = attention_forward(lin, cos, sin, mq, mk, table, seq_lengths)
     cot_pieces, cot_late = gather_plane(after(cot_own, *late), after(cot_y, *late), (mixed,))
     cot = jnp.concatenate(cot_pieces, axis=0)
 
@@ -898,7 +971,6 @@
     n2g.step().last()
     dw_up = dot_tn(after(normed_two, *n2g.second), gu_grad[:, units:]).astype(BF)
     n2g.here = after(n2g.here, dw_up)
-    normed_two_grad = n2g.own()
 
     def scattered(a):
         return lax.psum_scatter(a, "shard", scatter_dimension=0, tiled=True)
@@ -906,26 +978,21 @@
     dw_dt_own = scattered(dw_dt)
     dw_gate_own = scattered(dw_gate)
     dw_up_own = scattered(dw_up)
-    normed_two_grad = after(normed_two_grad, dw_dt_own)
+    n2g.here = after(n2g.here, dw_dt_own)
 
     def both_tp(own, other):
         first = t == 0
         return jnp.concatenate([jnp.where(first, own, other), jnp.where(first, other, own)], axis=0)[None]
 
-    def norm_back(rows, scale, gain, grad):
-        n = rows * scale
-        u = grad * gain
-        return scale * (u - n * jnp.mean(u * n, axis=-1, keepdims=True))
-
-    middle_grad = cot_own.astype(F32) + norm_back(middle, scale_two, gain_two, normed_two_grad)
+    *branch_own, middle_grad = norm_back(n2g, middle, gain_two, cot_own, 1)
 
     def rows_out(first_arrival):
         ffn.here = after(ffn.here, first_arrival)
         return ((middle + ffn.own()).astype(BF),)
 
     kept = []
-    branch_pieces, branch_late = gather_plane(
-        middle_grad.astype(BF), later=lambda c0: kept.extend(rows_out(c0)) or kept
+    branch_pieces, branch_late = gather_halves(
+        branch_own, later=lambda c0: kept.extend(rows_out(c0)) or kept
     )
     (out_own,) = kept
     dt_pieces = on_ctx(after(dw_dt_own, *branch_late))
@@ -933,7 +1000,7 @@
     out_other = to_y(out_own)
     mk_b = after(mk, dw_dt_own, dw_gate_own, out_own)
     n1g_away, n1g_here, dw_attn, d_low, dmq, dmk = attention_backward(
-        branch_pieces, w_eff, low_in, normed, mixed, shards, saved, cos, sin, mq, mk_b, perm, k, seq_lengths
+        branch_pieces, w_eff, low_in, normed, mixed, shards, saved, cos, sin, mq, mk_b, table, seq_lengths
     )
     n1g_away, n1g_here, *_ = lax.optimization_barrier((n1g_away, n1g_here, dt_pieces[2], gate_pieces[2], out_other))
     d_ups, d_out_down = d_low[: 3 * rank, : wide + 128], d_low[3 * rank :, wide + 128 :]
@@ -968,17 +1035,14 @@
     small_pieces = on_ctx(after(d_small_own, n1g.r1b))
     n1g.here = after(n1g.here, gate_grad)
 
-    normed_grad = n1g.own()
-    own_wide = rows_in.astype(F32)
-    in_own = middle_grad + norm_back(own_wide, scale_of(own_wide), gain_one, normed_grad)
-    in_low = after(in_own.astype(BF), dw_up_own)
-    in_first, in_second = to_y(in_low[: piece // 2]), to_y(in_low[piece // 2 :])
+    n1g.here = after(n1g.here, dw_up_own)
+    in_a, in_b = norm_back(n1g, rows_in, gain_one, middle_grad, 0)
+    in_first, in_second = to_y(in_a), to_y(in_b)
+    in_low = jnp.concatenate([in_a, in_b], axis=0)
     in_other = jnp.concatenate([in_first, in_second], axis=0)
     dw_attn_own = lax.psum_scatter(after(dw_attn, dw_up_own), "shard", scatter_dimension=0, tiled=True)[0]
-    dw_attn_own = after(dw_attn_own, in_first)
+    dw_attn_own = after(dw_attn_own, in_a)
     attn_pieces = on_ctx(dw_attn_own)
-    attn_pieces[2] = after(attn_pieces[2], in_second)
-    attn_pieces[3] = to_core(attn_pieces[2])
     input_grad = both_tp(in_low, after(in_other, attn_pieces[1])).astype(F32)
     outputs = both_tp(out_own, after(out_other, attn_pieces[1]))
 
@@ -986,7 +1050,7 @@
     w_in_eff_own = lax.dynamic_slice_in_dim(w_eff, s * ds, ds, 0)[:, : wide + 128]
     gain_one_own, gain_two_own = attn_gain.astype(F32), ffn_gain.astype(F32)
     d_gain_one = jnp.sum(w_in_eff_own.T.astype(F32) * dw_in_own.astype(F32), axis=0) / gain_one_own
-    products = lambda w, dw: jnp.sum(w.astype(F32) * after(dw, in_low).astype(F32), axis=1)
+    products = lambda w, dw: jnp.sum(w.astype(F32) * after(dw, in_a).astype(F32), axis=1)
     d_gain_two = (products(w_gu_own[:, :units], dw_gate_own) + products(w_gu_own[:, units:], dw_up_own)) / gain_two_own
     partial = jnp.concatenate(
         [
@@ -998,12 +1062,12 @@
         axis=0,
     )
     partial = partial + to_core(partial)
-    partial = after(partial, in_first)
+    partial = after(partial, attn_pieces[2])
     partial = partial + to_y(partial)
     partial_b = partial
     partial = partial + to_x(partial)
 
-    up_grad = place([after(p, in_other) for p in on_ctx(after(dw_up_own, n1g.r1b, n1g.r2a))], here)
+    up_grad = place([after(p, attn_pieces[1]) for p in on_ctx(after(dw_up_own, n1g.r1b, n1g.r2a))], here)
     query_weight_grad, key_weight_grad, value_weight_grad, out_weight_grad = place_heads(
         [after(p, up_grad, partial_b) for p in attn_pieces], here, wide
     )

time: 690 us -> 672 us (0.974)
  other arithmetic: 83.5 us -> 65.7 us
  waiting for transfers between devices: 180 us -> 169 us
  Pallas kernels: 168 us -> 177 us
    ppermute x22 -> x23, waiting for transfers between devices: 99.4 us -> 83.7 us  [to_y(): return lax.ppermute(a, 'tp', ALONG_Y)]
    pallas_call x0 -> x2, Pallas kernels: none -> 9.38 us  [norm_back(): pl.pallas_call(functools.partial(norm_back_kernel, side), grid=(2 * side,...]
    ppermute x26 -> x27, waiting for transfers between devices: 54.5 us -> 45.9 us  [to_x(): return lax.ppermute(a, 'ctx', ALONG_X)]
    all_gather x3, waiting for transfers between devices: 15.8 us -> 23.5 us  [gathered(): return lax.all_gather(a, 'shard', axis=0, tiled=True)]
    unnamed x192 -> x184, local copies, waits for them, and re-layouts: 46.1 us -> 51.6 us
    ppermute x22 -> x23, starting transfers between devices: 22.8 us -> 25.3 us  [to_y(): return lax.ppermute(a, 'tp', ALONG_Y)]
    ppermute x26 -> x27, starting transfers between devices: 27.7 us -> 29.3 us  [to_x(): return lax.ppermute(a, 'ctx', ALONG_X)]
  transfers between devices with their start and end apart: 93 -> 98, of which waited for: 31 -> 30; matrix products, arithmetic and copies ran while one was open for 33% -> 29% of each run, Pallas kernels for 24% -> 26%
where the time goes in v2:
time: 672 us; the launch traced here: 667 us
  Pallas kernels  177 us (26%)
  waiting for transfers between devices  169 us (25%)
  local copies, waits for them, and re-layouts  80.5 us (12%)
  matrix products  76.2 us (11%)
  starting transfers between devices  66.3 us (10%)
  other arithmetic  65.7 us (10%)
  between operations  16.6 us (2%)
  blocking collectives  15.7 us (2%)
    ppermute x23, waiting for transfers between devices, to_y(): return lax.ppermute(a, 'tp', ALONG_Y)  83.7 us
    pallas_call x1, Pallas kernels, attention_backward(): pl.pallas_call(functools.partial(backward_kernel, heads), grid_spec=grid,...  54.1 us
    unnamed x184, local copies, waits for them, and re-layouts  51.6 us
    ppermute x27, waiting for transfers between devices, to_x(): return lax.ppermute(a, 'ctx', ALONG_X)  45.9 us
    dot_general x4, matrix products, dot_tn(): lax.dot_general(a, b, (((0,), (0,)), ((), ())), preferred_element_type=F32)  45 us
    pallas_call x2, Pallas kernels, hidden_units_back(): pl.pallas_call(units_back_kernel, grid=(steps,), in_specs=in_specs, out_s...  39.8 us
    ppermute x27, starting transfers between devices, to_x(): return lax.ppermute(a, 'ctx', ALONG_X)  29.3 us
    ppermute x23, starting transfers between devices, to_y(): return lax.ppermute(a, 'tp', ALONG_Y)  25.3 us
  transfers between devices with their start and end apart: 98, of which 30 were waited for; matrix products, arithmetic and copies ran while one was open for 29% of the time, Pallas kernels for 26%

profile of v2, /device:TPU:0, one launch (start us, length us, event | category | flops | bytes accessed | tf_op | source)
XLA Modules:
  0.0 666.6 jit_solution(4780314364871394048)
XLA Ops:
  25.9 15.7 %all-gather = bf16[192,512]{1,0:T(8,128)(2,1)S(1)} all-gather(bf16[48,512]{1,0:T(8,128)(2,1)S(1)} %concatenate.87), channel_id=2, replica_groups=mesh['shard'=4,'ctx'=4,'tp'=2] {'shard'}, dimensions={0}, use_global_device_ids=true | all-gather | bytes 245760 | tf_op jit(solution)/shard_map/all_gather | solution.py:890
  79.9 9.8 %fusion.2.refs_18_ = bf16[2048,2048]{1,0:T(8,128)(2,1)} fusion(bf16[2048,2048]{1,0:T(8,128)(2,1)} %constant_dynamic-update-slice_fusion, f32[2048]{0:T(1024)S(1)} %bitcast.126, f32[2048]{0:T(1024)S(1)} %add_rsqrt_fusion), kind=kLoop, calls=%fused_computation.6 | loop fusion | flops 16777216 | bytes 16793600 | tf_op jit(solution)/shard_map/convert_element_type | solution.py:939
  92.3 9.6 %fusion.16.lin_ref = f32[2048,384]{1,0:T(8,128)} fusion(bf16[2048,2048]{1,0:T(8,128)(2,1)} %fusion.2.refs_18_, bf16[2048,640]{1,0:T(8,128)(2,1)S(1)} %add_convert_fusion.refs_16_), kind=kOutput, calls=%fused_computation.32 | convolution fusion | flops 3221225472 | bytes 13107200 | tf_op jit(solution)/shard_map/dot_general | solution.py:26
  101.9 24.8 %attention_forward.1 = (bf16[2048,256]{1,0:T(8,128)(2,1)S(1)}, f32[2048,256]{1,0:T(8,128)}, f32[2048,256]{1,0:T(8,128)}, bf16[2048,256]{1,0:T(8,128)(2,1)S(1)}, ...) custom-call(s32[24]{0:T(128)S(1)} %pad_add_fusion.perm.table, ...), custom_call_target="tpu_custom_call" | custom-call | flops 1048576 | bytes 65536 | tf_op jit(solution)/shard_map/attention_forward/pallas_call | solution.py:466
  132.5 9.9 %collective-permute-done.9 = bf16[128,2048]{1,0:T(8,128)(2,1)} collective-permute-done((bf16[128,2048]{1,0:T(8,128)(2,1)S(1)}, bf16[128,2048]{1,0:T(8,128)(2,1)}, u32[]{:S(2)}, u32[]{:S(2)}) %collective-permute-start.9) | collective-permute-done | bytes 524320 | tf_op jit(solution)/shard_map/ppermute | solution.py:46
  180.2 8.3 %collective-permute-done.15 = bf16[128,2048]{1,0:T(8,128)(2,1)S(1)} collective-permute-done((bf16[128,2048]{1,0:T(8,128)(2,1)S(1)}, bf16[128,2048]{1,0:T(8,128)(2,1)S(1)}, u32[]{:S(2)}, u32[]{:S(2)}) %collective-permute-start.15) | collective-permute-done | bytes 524320 | tf_op jit(solution)/shard_map/ppermute | solution.py:46
  199.1 18.6 %collective-permute-done.19 = bf16[256,2048]{1,0:T(8,128)(2,1)S(1)} collective-permute-done((bf16[256,2048]{1,0:T(8,128)(2,1)S(1)}, bf16[256,2048]{1,0:T(8,128)(2,1)S(1)}, u32[]{:S(2)}, u32[]{:S(2)}) %collective-permute-start.19) | collective-permute-done | bytes 1048608 | tf_op jit(solution)/shard_map/ppermute | solution.py:46
  237.7 24.4 %hidden_units.1 = (bf16[2048,1024]{1,0:T(8,128)(2,1)}, bf16[2048,1024]{1,0:T(8,128)(2,1)S(1)}, bf16[2048,1024]{1,0:T(8,128)(2,1)S(1)}) custom-call(bf16[2048,2048]{1,0:T(8,128)(2,1)} %constant_dynamic-update-slice_fusion.10.h_ref, bf16[2048,2048]{1,0:T(8,128)(2,1)} %all-gather.7.cloned.1.call-done.w_ref.w_gu_ref), custom_call_target="tpu_custom_call" | custom-call | flops 1048576 | bytes 65536 | tf_op jit(solution)/shard_map/hidden_units/pallas_call | solution.py:652
  266.2 14.0 %convolution_convert_fusion.4 = bf16[2048,1024]{1,0:T(8,128)(2,1)} fusion(bf16[2048,2048]{1,0:T(8,128)(2,1)} %copy-done.55, bf16[2048,1024]{1,0:T(8,128)(2,1)} %get-tuple-element.193), kind=kOutput, calls=%fused_computation.18 | convolution fusion | flops 8592031744 | bytes 16777216 | tf_op jit(solution)/shard_map/dot_general | solution.py:34
  280.2 23.5 %all-gather.9.cloned.1.call-done.w_dt_ref = bf16[2048,1024]{1,0:T(8,128)(2,1)} async-done(((bf16[512,1024]{1,0:T(8,128)(2,1)}), bf16[2048,1024]{1,0:T(8,128)(2,1)}) %all-gather.9.cloned.1.call-update) | async-done | bytes 4194320 | tf_op jit(solution)/shard_map/all_gather | solution.py:860
  303.6 9.4 %convolution_convert_fusion.2 = bf16[1024,2048]{1,0:T(8,128)(2,1)} fusion(bf16[2048,1024]{1,0:T(8,128)(2,1)} %all-gather.9.cloned.1.call-done.w_dt_ref, bf16[2048,1024]{1,0:T(8,128)(2,1)} %get-tuple-element.193), kind=kOutput, calls=%fused_computation.16 | convolution fusion | flops 4297064448 | bytes 10485760 | tf_op jit(solution)/shard_map/dot_general | solution.py:30
  328.6 20.5 %hidden_units_back.2 = (bf16[2048,2048]{1,0:T(8,128)(2,1)}, bf16[1024,2048]{1,0:T(8,128)(2,1)}) custom-call(bf16[2048,2048]{1,0:T(8,128)(2,1)} %copy-done.55, bf16[2048,1024]{1,0:T(8,128)(2,1)S(1)} %copy-done.25, bf16[2048,1024]{1,0:T(8,128)(2,1)} %copy-done.26, bf16[2048,1024]{1,0:T(8,128)(2,1)} %all-gather.9.cloned.1.call-done.w_dt_ref, ...), custom_call_target="tpu_custom_call" | custom-call | flops 12884901888 | bytes 25165824 | tf_op jit(solution)/shard_map/hidden_units_back/pallas_call | solution.py:695
  354.0 19.3 %hidden_units_back.3 = (bf16[2048,2048]{1,0:T(8,128)(2,1)}, bf16[1024,2048]{1,0:T(8,128)(2,1)S(1)}) custom-call(bf16[2048,2048]{1,0:T(8,128)(2,1)} %copy-done.55, bf16[2048,1024]{1,0:T(8,128)(2,1)S(1)} %copy-done.25, bf16[2048,1024]{1,0:T(8,128)(2,1)} %copy-done.26, ...), custom_call_target="tpu_custom_call", output_to_operand_aliasing={{0}: (5, {})} | custom-call | flops 12884901888 | bytes 25165824 | tf_op jit(solution)/shard_map/hidden_units_back/pallas_call | solution.py:695
  375.4 14.4 %fusion.7 = bf16[2048,1024]{1,0:T(8,128)(2,1)} fusion(bf16[2048,2048]{1,0:T(8,128)(2,1)} %constant_dynamic-update-slice_fusion.10.h_ref, bf16[2048,2048]{1,0:T(8,128)(2,1)} %get-tuple-element.209), kind=kOutput, calls=%fused_computation.12 | convolution fusion | flops 8592031744 | bytes 16777216 | tf_op jit(solution)/shard_map/dot_general | solution.py:34
  398.0 10.8 %collective-permute-done.40 = bf16[128,2048]{1,0:T(8,128)(2,1)S(1)} collective-permute-done((bf16[128,2048]{1,0:T(8,128)(2,1)S(1)}, bf16[128,2048]{1,0:T(8,128)(2,1)S(1)}, u32[]{:S(2)}, u32[]{:S(2)}) %collective-permute-start.40) | collective-permute-done | bytes 524320 | tf_op jit(solution)/shard_map/ppermute | solution.py:46
  414.4 14.0 %fusion.10 = bf16[2048,1024]{1,0:T(8,128)(2,1)} fusion(bf16[2048,2048]{1,0:T(8,128)(2,1)} %constant_dynamic-update-slice_fusion.10.h_ref, bf16[2048,2048]{1,0:T(8,128)(2,1)} %get-tuple-element.209), kind=kOutput, calls=%fused_computation.13 | convolution fusion | flops 8592031744 | bytes 16777216 | tf_op jit(solution)/shard_map/dot_general | solution.py:34
  447.5 8.4 %collective-permute-done.48.refs_2_ = bf16[128,2048]{1,0:T(8,128)(2,1)} collective-permute-done((bf16[128,2048]{1,0:T(8,128)(2,1)S(1)}, bf16[128,2048]{1,0:T(8,128)(2,1)}, u32[]{:S(2)}, u32[]{:S(2)}) %collective-permute-start.48) | collective-permute-done | bytes 524320 | tf_op jit(solution)/shard_map/ppermute | solution.py:42
  456.6 9.2 %collective-permute-done.51.refs_5_ = bf16[128,2048]{1,0:T(8,128)(2,1)} collective-permute-done((bf16[128,2048]{1,0:T(8,128)(2,1)}, bf16[128,2048]{1,0:T(8,128)(2,1)}, u32[]{:S(2)}, u32[]{:S(2)}) %collective-permute-start.51) | collective-permute-done | bytes 524320 | tf_op jit(solution)/shard_map/ppermute | solution.py:46
  468.0 8.5 %collective-permute-done.52.refs_6_ = bf16[128,2048]{1,0:T(8,128)(2,1)} collective-permute-done((bf16[128,2048]{1,0:T(8,128)(2,1)}, bf16[128,2048]{1,0:T(8,128)(2,1)}, u32[]{:S(2)}, u32[]{:S(2)}) %collective-permute-start.52) | collective-permute-done | bytes 524320 | tf_op jit(solution)/shard_map/ppermute | solution.py:46
  486.9 54.1 %attention_backward.1 = (bf16[1024,2048]{1,0:T(8,128)(2,1)}, bf16[1024,2048]{1,0:T(8,128)(2,1)}, bf16[4,640,512]{2,1,0:T(8,128)(2,1)}, f32[32,640]{1,0:T(8,128)S...) custom-call(s32[24]{0:T(128)S(1)} %pad_add_fusion.perm.table, s32[1]{0:T(128)} %copy.158.length, ...), custom_call_target="tpu_custom_call" | custom-call | flops 49999998976 | bytes 16777216 | tf_op jit(solution)/shard_map/attention_backward/pallas_call | solution.py:555
  564.0 7.8 %place.3 = f32[4096,512]{1,0:T(8,128)} custom-call(s32[1]{0:T(128)} %bitcast.34.at, bf16[512,1024]{1,0:T(8,128)(2,1)} %reduce-scatter.5.cloned.1.call-done.refs_0_, bf16[512,1024]{1,0:T(8,128)(2,1)} %collective-permute-done.64.refs_1_, bf16[512,1024]{1,0:T(8,128)(2,1)S(1)} %collective-permute-done.61.refs_2_, bf16[512,1024]{1,0:T(8,128)(2,1)} %collective-permute-done.65.refs_3_), custom_call_target="tpu_custom_call" | custom-call | bytes 25165824 | tf_op jit(solution)/shard_map/place/pallas_call | solution.py:739
  583.6 8.6 %place.4 = f32[512,4096]{1,0:T(8,128)} custom-call(s32[1]{0:T(128)} %bitcast.34.at, bf16[512,1024]{1,0:T(8,128)(2,1)S(1)} %copy-done.10, bf16[512,1024]{1,0:T(8,128)(2,1)} %collective-permute-done.71.refs_1_, bf16[512,1024]{1,0:T(8,128)(2,1)S(1)} %copy-done.15, bf16[512,1024]{1,0:T(8,128)(2,1)} %collective-permute-done.72.refs_3_), custom_call_target="tpu_custom_call" | custom-call | bytes 25165824 | tf_op jit(solution)/shard_map/place/pallas_call | solution.py:739
  595.4 9.2 %collective-permute-done.73.r1a = bf16[128,2048]{1,0:T(8,128)(2,1)} collective-permute-done((bf16[128,2048]{1,0:T(8,128)(2,1)}, bf16[128,2048]{1,0:T(8,128)(2,1)}, u32[]{:S(2)}, u32[]{:S(2)}) %collective-permute-start.73) | collective-permute-done | bytes 524320 | tf_op jit(solution)/shard_map/ppermute | solution.py:42
  632.7 8.4 %collective-permute-done.81.refs_2_ = bf16[640,512]{1,0:T(8,128)(2,1)S(1)} collective-permute-done((bf16[640,512]{1,0:T(8,128)(2,1)}, bf16[640,512]{1,0:T(8,128)(2,1)S(1)}, u32[]{:S(2)}, u32[]{:S(2)}) %collective-permute-start.81) | collective-permute-done | bytes 655392 | tf_op jit(solution)/shard_map/ppermute | solution.py:42
  (533 shorter events, 288.8 us)
Async XLA Ops:
  7.2 82.5 %all-gather.5.cloned.1.call-start = ((), (), s32[]{:S(2)}) async-start(), calls=%async_computation.4 | async-start | bytes 3276800 | tf_op jit(solution)/shard_map/all_gather | solution.py:860
  11.7 226.0 %all-gather.7.cloned.1.call-start = ((), (), s32[]{:S(2)}) async-start(), calls=%async_computation.5 | async-start | bytes 10485760 | tf_op jit(solution)/shard_map/all_gather | solution.py:860
  13.0 55.1 %collective-permute-start.3 = (bf16[256,2048]{1,0:T(8,128)(2,1)S(1)}, bf16[256,2048]{1,0:T(8,128)(2,1)}, u32[]{:S(2)}, u32[]{:S(2)}) collective-permute-start(bf16[256,2048]{1,0:T(8,128)(2,1)S(1)} %get-tuple-element.342.rows_ref), channel_id=1, source_target_pairs={{0,2},{2,0},{4,6},{6,4},{1,3},{3,1},{5,7},{7,5},{8,10},{10,8},{12,... | collective-permute-start | bytes 3145736 | tf_op jit(solution)/shard_map/ppermute | solution.py:38
  13.5 36.4 %collective-permute-start = (bf16[256,2048]{1,0:T(8,128)(2,1)S(1)}, bf16[256,2048]{1,0:T(8,128)(2,1)}, u32[]{:S(2)}, u32[]{:S(2)}) collective-permute-start(bf16[256,2048]{1,0:T(8,128)(2,1)S(1)} %get-tuple-element.342.rows_ref), channel_id=1, source_target_pairs={{0,4},{2,6},{4,0},{6,2},{1,5},{3,7},{5,1},{7,3},{8,12},{10,14},{12... | collective-permute-start | bytes 3145736 | tf_op jit(solution)/shard_map/ppermute | solution.py:42
  16.8 39.7 %collective-permute-start.2 = (bf16[128,2048]{1,0:T(8,128)(2,1)}, bf16[128,2048]{1,0:T(8,128)(2,1)S(1)}, u32[]{:S(2)}, u32[]{:S(2)}) collective-permute-start(bf16[128,2048]{1,0:T(8,128)(2,1)} %dynamic-slice_bitcast_fusion.2), channel_id=1, source_target_pairs={{0,4},{2,6},{4,0},{6,2},{1,5},{3,7},{5,1},{7,3},{8,12},{10,14},{12... | collective-permute-start | bytes 1572872 | tf_op jit(solution)/shard_map/ppermute | solution.py:42
  21.5 282.2 %all-gather.9.cloned.1.call-start = ((), (), s32[]{:S(2)}) async-start(), calls=%async_computation.6 | async-start | bytes 5242880 | tf_op jit(solution)/shard_map/all_gather | solution.py:860
  65.0 67.5 %collective-permute-start.10 = (bf16[128,2048]{1,0:T(8,128)(2,1)}, bf16[128,2048]{1,0:T(8,128)(2,1)}, u32[]{:S(2)}, u32[]{:S(2)}) collective-permute-start(bf16[128,2048]{1,0:T(8,128)(2,1)} %slice.438), channel_id=1, source_target_pairs={{0,4},{2,6},{4,0},{6,2},{1,5},{3,7},{5,1},{7,3},{8,12},{10,14},{12... | collective-permute-start | bytes 1572872 | tf_op jit(solution)/shard_map/ppermute | solution.py:42
  70.4 56.3 %collective-permute-start.8 = (bf16[256,2048]{1,0:T(8,128)(2,1)}, bf16[256,2048]{1,0:T(8,128)(2,1)}, u32[]{:S(2)}, u32[]{:S(2)}) collective-permute-start(bf16[256,2048]{1,0:T(8,128)(2,1)} %get-tuple-element.180.base_ref), channel_id=1, source_target_pairs={{0,4},{2,6},{4,0},{6,2},{1,5},{3,7},{5,1},{7,3},{8,12},{10,14},{12... | collective-permute-start | bytes 3145736 | tf_op jit(solution)/shard_map/ppermute | solution.py:42
  157.5 270.9 %reduce-scatter.5.cloned.1.call-start = ((), (), s32[]{:S(2)}) async-start(), calls=%async_computation.7 | async-start | bytes 5242880 | tf_op jit(solution)/shard_map/reduce_scatter | solution.py:976
  157.5 39.1 %collective-permute-start.27 = (bf16[256,2048]{1,0:T(8,128)(2,1)}, bf16[256,2048]{1,0:T(8,128)(2,1)S(1)}, u32[]{:S(2)}, u32[]{:S(2)}) collective-permute-start(bf16[256,2048]{1,0:T(8,128)(2,1)} %get-tuple-element.180.base_ref), channel_id=1, source_target_pairs={{0,2},{2,0},{4,6},{6,4},{1,3},{3,1},{5,7},{7,5},{8,10},{10,8},{12,... | collective-permute-start | bytes 3145736 | tf_op jit(solution)/shard_map/ppermute | solution.py:38
  198.9 34.0 %collective-permute-start.22 = (bf16[256,2048]{1,0:T(8,128)(2,1)S(1)}, bf16[256,2048]{1,0:T(8,128)(2,1)S(1)}, u32[]{:S(2)}, u32[]{:S(2)}) collective-permute-start(bf16[256,2048]{1,0:T(8,128)(2,1)S(1)} %get-tuple-element.336), channel_id=1, source_target_pairs={{0,2},{2,0},{4,6},{6,4},{1,3},{3,1},{5,7},{7,5},{8,10},{10,8},{12,... | collective-permute-start | bytes 3145736 | tf_op jit(solution)/shard_map/ppermute | solution.py:38
  313.1 167.3 %reduce-scatter.7.cloned.1.call-start = ((), (), s32[]{:S(2)}) async-start(), calls=%async_computation.8 | async-start | bytes 5242880 | tf_op jit(solution)/shard_map/reduce_scatter | solution.py:976
  327.6 47.8 %collective-permute-start.35 = (bf16[128,2048]{1,0:T(8,128)(2,1)S(1)}, bf16[128,2048]{1,0:T(8,128)(2,1)S(1)}, u32[]{:S(2)}, u32[]{:S(2)}) collective-permute-start(bf16[128,2048]{1,0:T(8,128)(2,1)S(1)} %get-tuple-element.196), channel_id=1, source_target_pairs={{0,4},{2,6},{4,0},{6,2},{1,5},{3,7},{5,1},{7,3},{8,12},{10,14},{12... | collective-permute-start | bytes 1572872 | tf_op jit(solution)/shard_map/ppermute | solution.py:42
  328.1 47.2 %collective-permute-start.38 = (bf16[128,2048]{1,0:T(8,128)(2,1)S(1)}, bf16[128,2048]{1,0:T(8,128)(2,1)S(1)}, u32[]{:S(2)}, u32[]{:S(2)}) collective-permute-start(bf16[128,2048]{1,0:T(8,128)(2,1)S(1)} %get-tuple-element.197), channel_id=1, source_target_pairs={{0,1},{1,0},{2,3},{3,2},{4,5},{5,4},{6,7},{7,6},{8,9},{9,8},{10,11... | collective-permute-start | bytes 1572872 | tf_op jit(solution)/shard_map/ppermute | solution.py:46
  349.1 41.0 %collective-permute-start.39 = (bf16[1024,2048]{1,0:T(8,128)(2,1)}, bf16[1024,2048]{1,0:T(8,128)(2,1)}, u32[]{:S(2)}, u32[]{:S(2)}) collective-permute-start(bf16[1024,2048]{1,0:T(8,128)(2,1)} %get-tuple-element.201), channel_id=1, source_target_pairs={{0,2},{2,0},{4,6},{6,4},{1,3},{3,1},{5,7},{7,5},{8,10},{10,8},{12,... | collective-permute-start | bytes 12582920 | tf_op jit(solution)/shard_map/ppermute | solution.py:38
  389.8 157.9 %reduce-scatter.9.cloned.1.call-start = ((), (), s32[]{:S(2)}) async-start(), calls=%async_computation.9 | async-start | bytes 5242880 | tf_op jit(solution)/shard_map/reduce_scatter | solution.py:976
  395.0 33.4 %collective-permute-start.42 = (bf16[128,2048]{1,0:T(8,128)(2,1)}, bf16[128,2048]{1,0:T(8,128)(2,1)S(1)}, u32[]{:S(2)}, u32[]{:S(2)}) collective-permute-start(bf16[128,2048]{1,0:T(8,128)(2,1)} %get-tuple-element.218), channel_id=1, source_target_pairs={{0,4},{2,6},{4,0},{6,2},{1,5},{3,7},{5,1},{7,3},{8,12},{10,14},{12... | collective-permute-start | bytes 1572872 | tf_op jit(solution)/shard_map/ppermute | solution.py:42
  396.6 32.7 %collective-permute-start.45 = (bf16[128,2048]{1,0:T(8,128)(2,1)}, bf16[128,2048]{1,0:T(8,128)(2,1)S(1)}, u32[]{:S(2)}, u32[]{:S(2)}) collective-permute-start(bf16[128,2048]{1,0:T(8,128)(2,1)} %get-tuple-element.219), channel_id=1, source_target_pairs={{0,1},{1,0},{2,3},{3,2},{4,5},{5,4},{6,7},{7,6},{8,9},{9,8},{10,11... | collective-permute-start | bytes 1572872 | tf_op jit(solution)/shard_map/ppermute | solution.py:46
  439.6 26.1 %collective-permute-start.50 = (bf16[128,2048]{1,0:T(8,128)(2,1)S(1)}, bf16[128,2048]{1,0:T(8,128)(2,1)S(1)}, u32[]{:S(2)}, u32[]{:S(2)}) collective-permute-start(bf16[128,2048]{1,0:T(8,128)(2,1)S(1)} %get-tuple-element.220.refs_0_), channel_id=1, source_target_pairs={{0,1},{1,0},{2,3},{3,2},{4,5},{5,4},{6,7},{7,6},{8,9},{9,8},{10,11... | collective-permute-start | bytes 1572872 | tf_op jit(solution)/shard_map/ppermute | solution.py:46
  466.7 155.1 %reduce-scatter.11.cloned.1.call-start = ((), (), s32[]{:S(2)}) async-start(), calls=%async_computation.10 | async-start | bytes 3276800 | tf_op jit(solution)/shard_map/reduce_scatter | solution.py:1043
  480.4 61.3 %collective-permute-start.47 = (bf16[256,2048]{1,0:T(8,128)(2,1)}, bf16[256,2048]{1,0:T(8,128)(2,1)S(1)}, u32[]{:S(2)}, u32[]{:S(2)}) collective-permute-start(bf16[256,2048]{1,0:T(8,128)(2,1)} %fusion.13), channel_id=1, source_target_pairs={{0,1},{1,0},{2,3},{3,2},{4,5},{5,4},{6,7},{7,6},{8,9},{9,8},{10,11... | collective-permute-start | bytes 3145736 | tf_op jit(solution)/shard_map/ppermute | solution.py:46
  481.9 59.8 %collective-permute-start.61 = (bf16[512,1024]{1,0:T(8,128)(2,1)}, bf16[512,1024]{1,0:T(8,128)(2,1)S(1)}, u32[]{:S(2)}, u32[]{:S(2)}) collective-permute-start(bf16[512,1024]{1,0:T(8,128)(2,1)} %reduce-scatter.5.cloned.1.call-done.refs_0_), channel_id=1, source_target_pairs={{0,4},{2,6},{4,0},{6,2},{1,5},{3,7},{5,1},{7,3},{8,12},{10,14},{12... | collective-permute-start | bytes 3145736 | tf_op jit(solution)/shard_map/ppermute | solution.py:42
  482.4 59.3 %collective-permute-start.62 = (bf16[512,1024]{1,0:T(8,128)(2,1)}, bf16[512,1024]{1,0:T(8,128)(2,1)S(1)}, u32[]{:S(2)}, u32[]{:S(2)}) collective-permute-start(bf16[512,1024]{1,0:T(8,128)(2,1)} %reduce-scatter.7.cloned.1.call-done.refs_0_), channel_id=1, source_target_pairs={{0,4},{2,6},{4,0},{6,2},{1,5},{3,7},{5,1},{7,3},{8,12},{10,14},{12... | collective-permute-start | bytes 3145736 | tf_op jit(solution)/shard_map/ppermute | solution.py:42
  594.1 36.9 %collective-permute-start.85 = (bf16[512,1024]{1,0:T(8,128)(2,1)S(1)}, bf16[512,1024]{1,0:T(8,128)(2,1)S(1)}, u32[]{:S(2)}, u32[]{:S(2)}) collective-permute-start(bf16[512,1024]{1,0:T(8,128)(2,1)S(1)} %copy-done.9), channel_id=1, source_target_pairs={{0,4},{2,6},{4,0},{6,2},{1,5},{3,7},{5,1},{7,3},{8,12},{10,14},{12... | collective-permute-start | bytes 3145736 | tf_op jit(solution)/shard_map/ppermute | solution.py:42
  (149 other events, 1956.6 us)
Sparse Core Ops, SparseCore 0:
  11.8 60.5 all-gather.4
  74.6 148.3 all-gather.6
  224.6 78.9 all-gather.8
  313.2 75.4 reduce-scatter.4
  390.9 77.2 reduce-scatter.6
  470.4 77.2 reduce-scatter.8
  550.1 52.6 reduce-scatter.10
